TPU v7x, 32 devices: a whole 2x2x4 slice. The times are simulated.
32 devices in a mesh: groups: 2 (over y), replica: 4 (over x, core), tensor: 4 (over z).
Axes of the slice: x: 2, y: 2, z: 4, core: 2. Of those that a mesh axis runs over, the one named last changes fastest.
Arguments:
- queries: bfloat16 [4096, 8192], P(('groups', 'replica', 'tensor')), parts along dimension 0, may hold values from -28 to 28
- keys: bfloat16 [4096, 32, 1024], P(('groups', 'replica', 'tensor')), parts along dimension 0, may hold values from -6 to 6
- values: bfloat16 [4096, 32, 1024], P(('groups', 'replica', 'tensor')), parts along dimension 0, may hold values from -6 to 6
- lengths: int32 [4096], P(('groups', 'replica', 'tensor')), parts along dimension 0, may hold values from 2 to 32, as said below
- output_projection_weight: bfloat16 [8192, 4096], P(None, 'tensor'), may hold values from -0.0625 to 0.0625
- adapter_down_factors: bfloat16 [96, 8192, 64], P(('groups', 'replica'), 'tensor'), parts along dimension 0, may hold values from -0.0625 to 0.0625
- adapter_up_factors: bfloat16 [96, 64, 4096], P(('groups', 'replica'), None, 'tensor'), parts along dimension 0, may hold values from -0.75 to 0.75
- block_adapter_index: int32 [32], P(('groups', 'replica')), parts along dimension 0, may hold values from 0 to 47
- block_live_rows: int32 [32], P(('groups', 'replica')), parts along dimension 0, may hold values from 1 to 128, as said below
- adapter_storage_slot: int32 [96], P('groups'), parts along dimension 0, may hold values from 0 to 47, each once
Outputs:
- projected: bfloat16 [4096, 4096], P(('groups', 'replica'), 'tensor'), parts along dimension 0
There are 2 independent parts, one for each index of `groups`. A program takes and returns all parts, laid end to end along the dimension named above; an argument that names none is the same for every part. Nothing has to cross between parts.
Inputs may be any that keep to these rules, and one draw needn't show every extreme that they name: `lengths`: some row has the full length 32. `block_live_rows`: the first block of each draw is full. Adapter a is stored at slot adapter_storage_slot[a], on replica adapter_storage_slot[a] // 12.
All inputs are finite; a program needn't handle non-finite values.
Results may differ from a plain program's by a relative error of at most 0.01.
Values may be sent and summed in bfloat16 or wider, within the bound.
No kernel may reach another device: no remote copies, remote signals or barrier semaphores. Data moves between devices by JAX's collectives and lax.ppermute only.
A program may use at most 192 MiB of HBM per device.

v0:
```python
import jax
import jax.numpy as jnp
from jax import lax
from jax.sharding import PartitionSpec as P

QUERY_HEAD_COUNT = 64
KVH = 8
HEAD_SIZE = 128


def body(
    queries,
    keys,
    values,
    lengths,
    output_projection_weight,
    adapter_down_factors,
    adapter_up_factors,
    block_adapter_index,
    block_live_rows,
    adapter_storage_slot,
):
    row_count = queries.shape[0]
    span = keys.shape[1]
    group_size = QUERY_HEAD_COUNT // KVH
    shard_index = lax.axis_index("tensor")
    query_heads = queries.reshape(row_count, KVH, group_size, HEAD_SIZE)
    key_heads = keys.reshape(row_count, span, KVH, HEAD_SIZE)
    value_heads = values.reshape(row_count, span, KVH, HEAD_SIZE).astype(jnp.float32)
    scores = jnp.einsum(
        "rkgd,rpkd->rkgp", query_heads, key_heads, preferred_element_type=jnp.float32
    ) * HEAD_SIZE ** (-0.5)
    visible = (jnp.arange(span)[None, :] < lengths[:, None])[:, None, None, :]
    scores = jnp.where(visible, scores, -1e30)
    highest = jnp.max(scores, axis=3, keepdims=True)
    weights = jnp.where(visible, jnp.exp(scores - highest), 0.0)
    totals = jnp.sum(weights, axis=3)
    summed = jnp.einsum("rkgp,rpkd->rkgd", weights, value_heads)
    local_attended = (
        (summed / totals[..., None])
        .reshape(row_count, QUERY_HEAD_COUNT * HEAD_SIZE)
        .astype(jnp.bfloat16)
    )
    attended = lax.all_gather(local_attended, "tensor", axis=0, tiled=True)
    replica_rows = attended.shape[0]
    base = jnp.dot(attended, output_projection_weight, preferred_element_type=jnp.float32)
    blocks = block_adapter_index.shape[0]
    wanted = adapter_storage_slot[block_adapter_index]
    replicas = lax.axis_size("replica")
    home_index = lax.axis_index("replica")
    adapt_local = adapter_down_factors.shape[0]
    requests = jnp.broadcast_to(wanted[None, :], (replicas, blocks))
    received = lax.all_to_all(requests, "replica", split_axis=0, concat_axis=0, tiled=True)
    owned = received // adapt_local == home_index
    local_slot = jnp.clip(received - home_index * adapt_local, 0, adapt_local - 1)
    served_a = jnp.where(
        owned[..., None, None], adapter_down_factors[local_slot], jnp.zeros((), jnp.bfloat16)
    )
    served_b = jnp.where(
        owned[..., None, None], adapter_up_factors[local_slot], jnp.zeros((), jnp.bfloat16)
    )
    fetched_a, fetched_b = (
        lax.all_to_all(served_a, "replica", split_axis=0, concat_axis=0, tiled=True),
        lax.all_to_all(served_b, "replica", split_axis=0, concat_axis=0, tiled=True),
    )
    selected_down_factor = jnp.sum(fetched_a.astype(jnp.float32), axis=0).astype(jnp.bfloat16)
    selected_up_factor = jnp.sum(fetched_b.astype(jnp.float32), axis=0).astype(jnp.bfloat16)
    input_width = adapter_down_factors.shape[1]
    columns = lax.dynamic_slice_in_dim(attended, shard_index * input_width, input_width, 1)
    blocked = columns.reshape(blocks, replica_rows // blocks, input_width)
    partial_rank = jnp.einsum(
        "bri,bik->brk", blocked, selected_down_factor, preferred_element_type=jnp.float32
    )
    reduced = lax.psum(partial_rank, "tensor").astype(jnp.bfloat16)
    delta = jnp.einsum(
        "brk,bkc->brc", reduced, selected_up_factor, preferred_element_type=jnp.float32
    )
    delta = delta.reshape(replica_rows, base.shape[1])
    live = (jnp.arange(replica_rows // blocks)[None, :] < block_live_rows[:, None]).reshape(
        replica_rows
    )
    return jnp.where(live[:, None], base + 2.0 * delta, 0.0).astype(jnp.bfloat16)


def solution(mesh):
    placed = (
        P(("groups", "replica", "tensor"), None),
        P(("groups", "replica", "tensor"), None, None),
        P(("groups", "replica", "tensor"), None, None),
        P(("groups", "replica", "tensor")),
        P(None, "tensor"),
        P(("groups", "replica"), "tensor", None),
        P(("groups", "replica"), None, "tensor"),
        P(("groups", "replica")),
        P(("groups", "replica")),
        P("groups"),
    )
    return jax.shard_map(
        body,
        mesh=mesh,
        in_specs=placed,
        out_specs=P(("groups", "replica"), "tensor"),
        check_vma=False,
    )
```

profile of v0, /device:TPU:0, one launch (start us, length us, event | category | flops | bytes accessed | tf_op | source)
XLA Modules:
  0.0 226.6 jit_solution(3926754458750381460)
XLA Ops:
  6.5 0.0 copy-start
  6.5 0.0 all-gather.2.cloned.1.call-start
  6.5 0.9 iota_compare_fusion
  7.4 2.2 copy.22
  9.7 7.0 %fusion.6 = (f32[128,8,8]{2,1,0:T(8,128)S(1)}, f32[128,8,8,32]{3,2,1,0:T(8,128)S(1)}) fusion(pred[128,32]{1,0:T(8,128)(4,1)S(1)} %iota_compare_fusion, bf16[128,8,8,128]{3,2,1,0:T(8,128)(2,1)S(1)} %bitcast.54, bf16[128,32,1024]{2,1,0:T(8,128)(2,1)} %param.11), kind=kOutput, calls=%fused_computation.13 | convolution fusion | flops 67887104 | bytes 11571200 | tf_op jit(solution)/shard_map/rkgd,rpkd->rkgp/dot_general | solution.py:30
  16.6 3.1 %fusion.7 = f32[128,8,8]{2,1,0:T(8,128)S(1)} fusion(f32[128,8,8,32]{3,2,1,0:T(8,128)S(1)} %get-tuple-element.8, f32[128,8,8]{2,1,0:T(8,128)S(1)} %get-tuple-element.7, pred[128,32]{1,0:T(8,128)(4,1)S(1)} %iota_compare_fusion), kind=kLoop, calls=%fused_computation.14 | loop fusion | flops 1302528 | bytes 1118208 | tf_op jit(solution)/shard_map/reduce_sum | solution.py:37
  19.7 5.9 %divide_convert_fusion = bf16[128,8,8,128]{3,2,1,0:T(8,128)(2,1)S(1)} fusion(f32[128,8,8]{2,1,0:T(8,128)S(1)} %fusion.7, f32[128,8,8,32]{3,2,1,0:T(8,128)S(1)} %get-tuple-element.8, f32[128,8,8]{2,1,0:T(8,128)S(1)} %get-tuple-element.7, pred[128,32]{1,0:T(8,128)(4,1)S(1)} %iota_compare_fusion, bf16[128,32,1024]{2,1,0:T(8,128)(2,1)} %param.12), kind=kOutput, calls=%fused_computation.9 | convolution fusion | flops 70254592 | bytes 11603968 | tf_op jit(solution)/shard_map/rkgp,rpkd->rkgd/dot_general | solution.py:38
  25.6 0.0 copy-start.3
  25.6 0.0 copy-start.2
  25.6 3.1 %copy.38 = bf16[16,8,64,128]{3,1,2,0:T(8,128)(2,1)} copy(bf16[16,8,64,128]{3,2,1,0:T(8,128)(2,1)S(1)} %bitcast.56) | data formatting | bytes 4194304
  28.8 0.0 all-gather.2.cloned.1.call-update
  28.8 0.0 copy-done.3
  28.8 0.0 copy-done.2
  28.8 0.6 gather_fusion
  29.5 0.6 broadcast_in_dim.79
  30.1 4.2 %all-to-all-start = ((s32[4,1,4]{2,1,0:T(1,128)}), s32[4,1,4]{2,1,0:T(1,128)S(1)}, u32[]{:S(2)}, u32[]{:S(2)}) async-start(s32[4,1,4]{2,1,0:T(1,128)} %broadcast_in_dim.79), calls=%async_computation | async-start | bytes 4096 | tf_op jit(solution)/shard_map/all_to_all | solution.py:53
  34.3 3.7 %all-to-all-done = s32[4,1,4]{2,1,0:T(1,128)S(1)} async-done(((s32[4,1,4]{2,1,0:T(1,128)}), s32[4,1,4]{2,1,0:T(1,128)S(1)}, u32[]{:S(2)}, u32[]{:S(2)}) %all-to-all-start) | async-done | bytes 96 | tf_op jit(solution)/shard_map/all_to_all | solution.py:53
  38.0 0.1 reshape.127
  38.1 3.6 %gather_fusion.2 = bf16[16,64,1024]{2,1,0:T(8,128)(2,1)} fusion(bf16[12,64,1024]{2,1,0:T(8,128)(2,1)} %param.16, s32[1024]{0:T(1024)S(1)} %pad_clamp_fusion), kind=kCustom, calls=%fused_computation.2 | custom fusion | bytes 4194368 | tf_op jit(solution)/shard_map/gather | solution.py:60
  41.7 3.2 %broadcast_select_fusion.1 = bf16[4,4,64,1024]{3,2,1,0:T(8,128)(2,1)} fusion(bf16[4,4,64,1024]{3,2,1,0:T(8,128)(2,1)} %bitcast.52, pred[4,4]{1,0:T(4,128)(4,1)S(1)} %fusion.18), kind=kLoop, calls=%fused_computation.23 | loop fusion | flops 1048576 | bytes 4194320 | tf_op jit(solution)/shard_map/jit(_where)/select_n | solution.py:59
  44.9 4.4 %all-to-all-start.2 = ((bf16[4,4,64,1024]{3,2,1,0:T(8,128)(2,1)}), bf16[4,4,64,1024]{3,2,1,0:T(8,128)(2,1)}, u32[]{:S(2)}, u32[]{:S(2)}) async-start(bf16[4,4,64,1024]{3,2,1,0:T(8,128)(2,1)} %broadcast_select_fusion.1), calls=%async_computation.2 | async-start | bytes 4194304 | tf_op jit(solution)/shard_map/all_to_all | solution.py:64
  49.4 0.0 copy-done
  49.4 2.8 %gather_fusion.1 = bf16[16,2048,64]{1,2,0:T(8,128)(2,1)} fusion(bf16[12,2048,64]{1,2,0:T(8,128)(2,1)S(1)} %copy-done, s32[1024]{0:T(1024)S(1)} %pad_clamp_fusion), kind=kCustom, calls=%fused_computation.1 | custom fusion | bytes 8388672 | tf_op jit(solution)/shard_map/gather | solution.py:57
  52.2 4.5 %broadcast_select_fusion = bf16[4,4,2048,64]{2,3,1,0:T(8,128)(2,1)} fusion(bf16[4,4,2048,64]{2,3,1,0:T(8,128)(2,1)} %bitcast.50, pred[4,4]{1,0:T(4,128)(4,1)S(1)} %fusion.18), kind=kLoop, calls=%fused_computation.12 | loop fusion | flops 2097152 | bytes 8388624 | tf_op jit(solution)/shard_map/jit(_where)/select_n | solution.py:56
  56.7 0.0 copy-start.4
  56.7 18.5 %all-to-all-done.2 = bf16[4,4,64,1024]{3,2,1,0:T(8,128)(2,1)} async-done(((bf16[4,4,64,1024]{3,2,1,0:T(8,128)(2,1)}), bf16[4,4,64,1024]{3,2,1,0:T(8,128)(2,1)}, u32[]{:S(2)}, u32[]{:S(2)}) %all-to-all-start.2) | async-done | bytes 2097184 | tf_op jit(solution)/shard_map/all_to_all | solution.py:64
  75.1 4.9 %all-to-all-start.1 = ((bf16[4,4,2048,64]{2,3,1,0:T(8,128)(2,1)}), bf16[4,4,2048,64]{2,3,1,0:T(8,128)(2,1)}, u32[]{:S(2)}, u32[]{:S(2)}) async-start(bf16[4,4,2048,64]{2,3,1,0:T(8,128)(2,1)} %broadcast_select_fusion), calls=%async_computation.1 | async-start | bytes 8388608 | tf_op jit(solution)/shard_map/all_to_all | solution.py:63
  80.0 0.0 copy-done.4
  80.1 0.1 fusion.19
  80.1 2.9 %reduce_sum.35 = bf16[4,64,1024]{2,1,0:T(8,128)(2,1)} reduce(bf16[4,4,64,1024]{3,2,1,0:T(8,128)(2,1)} %all-to-all-done.2, bf16[]{:T(256)} %constant.42.clone.1), dimensions={0}, to_apply=%region_4.5 | reduce | flops 786432 | bytes 2621442 | tf_op jit(solution)/shard_map/reduce_sum | solution.py:67
  83.1 45.2 %all-to-all-done.1 = bf16[4,4,2048,64]{2,3,1,0:T(8,128)(2,1)} async-done(((bf16[4,4,2048,64]{2,3,1,0:T(8,128)(2,1)}), bf16[4,4,2048,64]{2,3,1,0:T(8,128)(2,1)}, u32[]{:S(2)}, u32[]{:S(2)}) %all-to-all-start.1) | async-done | bytes 4194336 | tf_op jit(solution)/shard_map/all_to_all | solution.py:63
  128.3 3.1 %reduce_sum.34 = bf16[4,2048,64]{1,2,0:T(8,128)(2,1)S(1)} reduce(bf16[4,4,2048,64]{2,3,1,0:T(8,128)(2,1)} %all-to-all-done.1, bf16[]{:T(256)} %constant.42.clone.1), dimensions={0}, to_apply=%region_2.3 | reduce | flops 1572864 | bytes 5242882 | tf_op jit(solution)/shard_map/reduce_sum | solution.py:66
  131.4 49.9 %all-gather.2.cloned.1.call-done = bf16[512,8192]{1,0:T(8,128)(2,1)} async-done(((bf16[128,8192]{1,0:T(8,128)(2,1)}), bf16[512,8192]{1,0:T(8,128)(2,1)}) %all-gather.2.cloned.1.call-update) | async-done | bytes 8388624 | tf_op jit(solution)/shard_map/all_gather | solution.py:44
  181.3 1.8 constant_dynamic-slice_fusion
  183.1 0.8 fusion.23
  184.0 18.5 %all-reduce.1 = bf16[4,128,64]{1,2,0:T(8,128)(2,1)S(1)} all-reduce(f32[4,128,64]{1,2,0:T(8,128)S(1)} %fusion.23), channel_id=1, replica_groups=mesh['groups'=2,'replica'=4,'tensor'=4] {'tensor'}, use_global_device_ids=true, to_apply=%region_3.4 | all-reduce | flops 32768 | bytes 196608 | tf_op jit(solution)/shard_map/psum | solution.py:74
  202.5 1.5 convolution_multiply_fusion
  204.0 0.0 copy-start.1
  204.0 15.7 %fusion.9 = bf16[512,1024]{1,0:T(8,128)(2,1)} fusion(f32[4,128,1024]{2,1,0:T(8,128)S(1)} %convolution_multiply_fusion, bf16[512,8192]{1,0:T(8,128)(2,1)} %all-gather.2.cloned.1.call-done, bf16[8192,1024]{1,0:T(8,128)(2,1)} %param.14, pred[512]{0:T(512)(128)(4,1)S(1)} %fusion.19), kind=kOutput, calls=%fused_computation.18 | convolution fusion | flops 8591507456 | bytes 28312064 | tf_op jit(solution)/shard_map/dot_general | solution.py:46
  219.7 0.0 copy-done.1
  (7 shorter events, 0.1 us)
Async XLA Ops:
  6.5 42.8 %copy-start = (bf16[12,2048,64]{1,2,0:T(8,128)(2,1)S(1)}, bf16[12,2048,64]{1,2,0:T(8,128)(2,1)}, u32[]{:S(2)}) copy-start(bf16[12,2048,64]{1,2,0:T(8,128)(2,1)} %param.15) | copy-start | bytes 9437188
  6.5 174.8 %all-gather.2.cloned.1.call-start = ((), (), s32[]{:S(2)}) async-start(), calls=%async_computation.3 | async-start | bytes 10485760 | tf_op jit(solution)/shard_map/all_gather | solution.py:44
  25.6 3.2 %copy-start.3 = (s32[4]{0:T(128)S(1)}, s32[4]{0:T(128)}, u32[]{:S(2)}) copy-start(s32[4]{0:T(128)} %param.17) | copy-start | bytes 52
  25.6 3.2 %copy-start.2 = (s32[48]{0:T(128)S(1)}, s32[48]{0:T(128)}, u32[]{:S(2)}) copy-start(s32[48]{0:T(128)} %param.19) | copy-start | bytes 580
  30.1 7.9 %all-to-all-start = ((s32[4,1,4]{2,1,0:T(1,128)}), s32[4,1,4]{2,1,0:T(1,128)S(1)}, u32[]{:S(2)}, u32[]{:S(2)}) async-start(s32[4,1,4]{2,1,0:T(1,128)} %broadcast_in_dim.79), calls=%async_computation | async-start | bytes 4096 | tf_op jit(solution)/shard_map/all_to_all | solution.py:53
  44.9 30.2 %all-to-all-start.2 = ((bf16[4,4,64,1024]{3,2,1,0:T(8,128)(2,1)}), bf16[4,4,64,1024]{3,2,1,0:T(8,128)(2,1)}, u32[]{:S(2)}, u32[]{:S(2)}) async-start(bf16[4,4,64,1024]{3,2,1,0:T(8,128)(2,1)} %broadcast_select_fusion.1), calls=%async_computation.2 | async-start | bytes 4194304 | tf_op jit(solution)/shard_map/all_to_all | solution.py:64
  56.7 23.4 %copy-start.4 = (s32[4]{0:T(128)S(1)}, s32[4]{0:T(128)}, u32[]{:S(2)}) copy-start(s32[4]{0:T(128)} %param.18) | copy-start | bytes 52
  75.1 53.1 %all-to-all-start.1 = ((bf16[4,4,2048,64]{2,3,1,0:T(8,128)(2,1)}), bf16[4,4,2048,64]{2,3,1,0:T(8,128)(2,1)}, u32[]{:S(2)}, u32[]{:S(2)}) async-start(bf16[4,4,2048,64]{2,3,1,0:T(8,128)(2,1)} %broadcast_select_fusion), calls=%async_computation.1 | async-start | bytes 8388608 | tf_op jit(solution)/shard_map/all_to_all | solution.py:63
  204.0 15.7 %copy-start.1 = (bf16[12,2048,64]{1,2,0:T(8,128)(2,1)S(1)}, bf16[12,2048,64]{1,2,0:T(8,128)(2,1)}, u32[]{:S(2)}) copy-start(bf16[12,2048,64]{1,2,0:T(8,128)(2,1)} %param.15) | copy-start | bytes 9437188
Sparse Core Ops, SparseCore 0:
  28.9 152.3 all-gather.1
where the time goes:
time: 227 us
  waiting for transfers between devices  117 us (52%)
  matrix products  30.9 us (14%)
  blocking collectives  18.5 us (8%)
  other arithmetic  17.9 us (8%)
  local copies, waits for them, and re-layouts  14.9 us (7%)
  between operations  13.6 us (6%)
  starting transfers between devices  13.5 us (6%)
    all_gather x1, waiting for transfers between devices, body(): attended = lax.all_gather(local_attended, 'tensor', axis=0, tiled=True)  49.9 us
    all_to_all x1, waiting for transfers between devices, body(): lax.all_to_all(served_a, 'replica', split_axis=0, concat_axis=0, tiled=True)  45.2 us
    psum x1, blocking collectives, body(): reduced = lax.psum(partial_rank, 'tensor').astype(jnp.bfloat16)  18.5 us
    all_to_all x1, waiting for transfers between devices, body(): lax.all_to_all(served_b, 'replica', split_axis=0, concat_axis=0, tiled=True)  18.5 us
    dot_general x1, matrix products, body(): jnp.dot(attended, output_projection_weight, preferred_element_type=jnp.fl...  15.7 us
    dot_general x1, matrix products, body(): jnp.einsum('rkgd,rpkd->rkgp', query_heads, key_heads, preferred_element_t...  6.96 us
    dot_general x1, matrix products, body(): summed = jnp.einsum('rkgp,rpkd->rkgd', weights, value_heads)  5.87 us
    unnamed x12, local copies, waits for them, and re-layouts  5.41 us
  transfers between devices with their start and end apart: 4, of which 4 were waited for; matrix products, arithmetic and copies ran while one was open for 10% of the time, Pallas kernels for 0%

commit v1 on v0

v1 whole, which is shorter than its diff:
```python
import functools

import jax
import jax.numpy as jnp
from jax import lax
from jax.experimental import pallas as pl
from jax.experimental.pallas import tpu as pltpu
from jax.sharding import PartitionSpec as P

QUERY_HEAD_COUNT = 64
KVH = 8
HEAD_SIZE = 128
LINE = 4
PARTS = 2
ANY = pl.BlockSpec(memory_space=pl.ANY)
SMEM = pl.BlockSpec(memory_space=pltpu.SMEM)
VMEM = pl.BlockSpec(memory_space=pltpu.VMEM)
BIG = pltpu.CompilerParams(vmem_limit_bytes=40 * 2**20)


def attention(queries, keys, values, lengths):
    row_count = queries.shape[0]
    span = keys.shape[1]
    group_size = QUERY_HEAD_COUNT // KVH
    query_heads = queries.reshape(row_count, KVH, group_size, HEAD_SIZE)
    key_heads = keys.reshape(row_count, span, KVH, HEAD_SIZE)
    value_heads = values.reshape(row_count, span, KVH, HEAD_SIZE).astype(jnp.float32)
    scores = jnp.einsum(
        "rkgd,rpkd->rkgp", query_heads, key_heads, preferred_element_type=jnp.float32
    ) * HEAD_SIZE ** (-0.5)
    visible = (jnp.arange(span)[None, :] < lengths[:, None])[:, None, None, :]
    scores = jnp.where(visible, scores, -1e30)
    highest = jnp.max(scores, axis=3, keepdims=True)
    weights = jnp.where(visible, jnp.exp(scores - highest), 0.0)
    totals = jnp.sum(weights, axis=3)
    summed = jnp.einsum("rkgp,rpkd->rkgd", weights, value_heads)
    return (
        (summed / totals[..., None])
        .reshape(row_count, QUERY_HEAD_COUNT * HEAD_SIZE)
        .astype(jnp.bfloat16)
    )


def slot_of(replicas, ids_ref, slots_ref, here, target, b):
    return slots_ref[ids_ref[lax.rem(target - here + replicas, replicas), b]]


def factor_copies(act, at, down_ref, up_ref, target, sems):
    depth = down_ref.shape[2]
    act(pltpu.make_async_copy(down_ref.at[at], target.at[:, pl.ds(0, depth)], sems.at[0]))
    act(pltpu.make_async_copy(up_ref.at[at], target.at[:, pl.ds(depth, up_ref.shape[2])], sems.at[1]))


def pair_kernel(replicas, blocks, here_ref, ids_ref, slots_ref, down_ref, up_ref, out_ref, sems):
    own = down_ref.shape[0]
    pairs = replicas // 2
    here = here_ref[0]
    pair, core = lax.div(here, 2), lax.rem(here, 2)

    def each(act):
        for k in range(pairs):
            target = lax.rem(pair + k, pairs) * 2 + 1 - core
            for b in range(blocks):
                slot = slot_of(replicas, ids_ref, slots_ref, here, target, b)

                @pl.when(lax.div(slot, own) == here)
                def _():
                    factor_copies(
                        act, lax.rem(slot, own), down_ref, up_ref, out_ref.at[k, b], sems.at[k, b]
                    )

    each(lambda copy: copy.start())
    each(lambda copy: copy.wait())


def merge_kernel(
    replicas, blocks, here_ref, ids_ref, slots_ref, down_ref, up_ref, paired_ref, out_ref, sems
):
    own = down_ref.shape[0]
    pairs = replicas // 2
    here = here_ref[0]
    pair, core = lax.div(here, 2), lax.rem(here, 2)

    def each(act):
        for k in range(1, pairs):
            target = lax.rem(pair + k, pairs) * 2 + core
            for b in range(blocks):
                slot = slot_of(replicas, ids_ref, slots_ref, here, target, b)
                home = lax.div(slot, own)
                place = out_ref.at[k - 1, b]

                @pl.when(home == here)
                def _():
                    factor_copies(
                        act, lax.rem(slot, own), down_ref, up_ref, place, sems.at[k - 1, b]
                    )

                @pl.when(home == pair * 2 + 1 - core)
                def _():
                    act(pltpu.make_async_copy(paired_ref.at[k, b], place, sems.at[k - 1, b, 0]))

    each(lambda copy: copy.start())
    each(lambda copy: copy.wait())


def pick_kernel(
    replicas,
    blocks,
    here_ref,
    ids_ref,
    slots_ref,
    order_ref,
    down_ref,
    up_ref,
    paired_ref,
    *refs,
):
    out_ref, sems = refs[-2:]
    fetched = refs[:-2]
    own = down_ref.shape[0]
    pairs = replicas // 2
    here = here_ref[0]
    pair = lax.div(here, 2)

    def each(act):
        for i in range(blocks):
            b = order_ref[i]
            slot = slots_ref[ids_ref[0, b]]
            home = lax.div(slot, own)
            shift = lax.rem(pair - lax.div(home, 2) + pairs, pairs)

            @pl.when(home == here)
            def _():
                factor_copies(act, lax.rem(slot, own), down_ref, up_ref, out_ref.at[i], sems.at[i])

            @pl.when((shift == 0) & (home != here))
            def _():
                act(pltpu.make_async_copy(paired_ref.at[0, b], out_ref.at[i], sems.at[i, 0]))

            for k in range(1, pairs):

                @pl.when(shift == k)
                def _():
                    act(pltpu.make_async_copy(fetched[k - 1].at[b], out_ref.at[i], sems.at[i, 0]))

    each(lambda copy: copy.start())
    each(lambda copy: copy.wait())


def pair_factors(down, up, ids, slots):
    replicas = lax.axis_size("replica")
    here = lax.axis_index("replica").astype(jnp.int32)[None]
    blocks = ids.shape[0]
    all_ids = jnp.stack(
        [ids]
        + [
            lax.ppermute(ids, "replica", [(i, (i - shift) % replicas) for i in range(replicas)])
            for shift in range(1, replicas)
        ]
    )
    pairs = replicas // 2
    piece = (blocks, down.shape[1], down.shape[2] + up.shape[2])
    packed = pl.pallas_call(
        functools.partial(pair_kernel, replicas, blocks),
        out_shape=jax.ShapeDtypeStruct((pairs,) + piece, down.dtype),
        in_specs=[SMEM] * 3 + [ANY] * 2,
        out_specs=VMEM,
        scratch_shapes=[pltpu.SemaphoreType.DMA((pairs, blocks, 2))],
        compiler_params=BIG,
    )(here, all_ids, slots, down, up)
    return here, all_ids, packed


def merge_factors(here, all_ids, slots, down, up, packed):
    replicas = lax.axis_size("replica")
    pairs, blocks = packed.shape[:2]
    paired = lax.ppermute(packed, "replica", [(i, i ^ 1) for i in range(replicas)])
    merged = pl.pallas_call(
        functools.partial(merge_kernel, replicas, blocks),
        out_shape=jax.ShapeDtypeStruct((pairs - 1,) + packed.shape[1:], down.dtype),
        in_specs=[SMEM] * 3 + [ANY] * 3,
        out_specs=VMEM,
        scratch_shapes=[pltpu.SemaphoreType.DMA((pairs - 1, blocks, 2))],
        compiler_params=BIG,
    )(here, all_ids, slots, down, up, paired)
    return paired, merged


def fetch_factors(merged):
    replicas = lax.axis_size("replica")
    return [
        lax.ppermute(
            merged[k - 1], "replica", [(i, (i + 2 * k) % replicas) for i in range(replicas)]
        )
        for k in range(1, replicas // 2)
    ]


def pick_factors(here, all_ids, slots, order, down, up, paired, fetched):
    replicas = lax.axis_size("replica")
    blocks = all_ids.shape[1]
    return pl.pallas_call(
        functools.partial(pick_kernel, replicas, blocks),
        out_shape=jax.ShapeDtypeStruct(paired.shape[1:], down.dtype),
        in_specs=[SMEM] * 4 + [ANY] * (3 + len(fetched)),
        out_specs=VMEM,
        scratch_shapes=[pltpu.SemaphoreType.DMA((blocks, 2))],
        compiler_params=BIG,
    )(here, all_ids, slots, order, down, up, paired, *fetched)


def sum_over_tensor(partial):
    size = lax.axis_size("tensor")
    if size != LINE:
        return lax.psum(partial, "tensor")
    for bit in (1, 2):
        partial = partial + lax.ppermute(
            partial, "tensor", [(i, i ^ bit) for i in range(size)]
        )
    return partial


def finish_kernel(order_ref, live_ref, end_ref, near_ref, far_ref, *refs):
    lasts = refs[:PARTS]
    sent_ref = refs[PARTS]
    passed_lasts = refs[PARTS + 1 : 2 * PARTS + 1]
    reduced_ref, factors_ref, result_ref = refs[2 * PARTS + 1 :]
    blocks = reduced_ref.shape[0]
    rows = near_ref.shape[0] // blocks
    depth = factors_ref.shape[2] - near_ref.shape[1]
    at_end = end_ref[0] == 1
    for i in range(blocks):
        b = order_ref[i]
        delta = lax.dot_general(
            reduced_ref[i],
            factors_ref[i, :, depth:],
            (((0,), (0,)), ((), ())),
            preferred_element_type=jnp.float32,
        )
        if i < 3:
            other = far_ref[pl.ds(i * rows, rows), :]
        else:
            other = jnp.concatenate([ref[...] for ref in lasts])
        if i > 0:
            if i < 3:
                passed = sent_ref[pl.ds((i - 1) * rows, rows), :]
            else:
                passed = jnp.concatenate([ref[...] for ref in passed_lasts])
            other = jnp.where(at_end, passed.astype(jnp.float32), other)
        total = near_ref[pl.ds(i * rows, rows), :] + other + 2.0 * delta
        live = lax.broadcasted_iota(jnp.int32, total.shape, 0) < live_ref[b]
        result_ref[pl.ds(pl.multiple_of(b * rows, rows), rows), :] = jnp.where(
            live, total, 0.0
        ).astype(result_ref.dtype)


def dot(a, b):
    return jnp.dot(a, b, preferred_element_type=jnp.float32)


def tie(*arrays):
    return lax.optimization_barrier(arrays)


def line_body(
    queries,
    keys,
    values,
    lengths,
    weight,
    down,
    up,
    ids,
    live_rows,
    slots,
):
    rows, width = queries.shape
    half = width // 2
    me = lax.axis_index("tensor")
    side = me // 2
    is_end = (me == 0) | (me == LINE - 1)
    near_at, far_at = side * half, (1 - side) * half
    ends = [(0, 1), (1, 0), (2, 3), (3, 2)]
    middle = [(1, 2), (2, 1)]
    outward = [(1, 0), (2, 3)]
    inward = [(0, 1), (3, 2)]
    order = jnp.array([[0, 1, 2, 3], [1, 0, 2, 3], [2, 3, 1, 0], [3, 2, 1, 0]], jnp.int32)[me]

    planes = lax.axis_size("groups") * lax.axis_size("replica")
    share = half // planes
    mine = lax.axis_index("groups") * lax.axis_size("replica") + lax.axis_index("replica")
    piece = lax.dynamic_slice_in_dim(weight, far_at + mine * share, share, 0)
    piece = lax.ppermute(piece, "tensor", inward)
    here, all_ids, packed = pair_factors(down, up, ids, slots)

    cut = rows // PARTS
    attended = attention(queries, keys, values, lengths)
    attended, packed = tie(attended, packed)
    piece, _ = tie(piece, attended)
    end_weight = lax.all_gather(piece, ("groups", "replica"), axis=0, tiled=True)
    near = lax.dynamic_slice_in_dim(attended, near_at, half, 1)
    far = lax.dynamic_slice_in_dim(attended, far_at, half, 1)
    nears = [near[p * cut : (p + 1) * cut] for p in range(PARTS)]
    fars = [far[p * cut : (p + 1) * cut] for p in range(PARTS)]
    e1, e2, e3, m1, m2, m3, m4 = ([] for _ in range(7))
    for p in range(PARTS):
        outer, inner = tie(jnp.where(is_end, fars[p], nears[p]), fars[p])
        e1.append(lax.ppermute(outer, "tensor", ends))
        m1.append(lax.ppermute(inner, "tensor", middle))
    paired, merged = merge_factors(here, all_ids, slots, down, up, packed)
    m1[0], merged = tie(m1[0], merged)
    fetched = fetch_factors(merged)
    for p in range(PARTS):
        outer, inner = tie(jnp.where(is_end, nears[p], m1[p]), e1[p])
        e2.append(lax.ppermute(outer, "tensor", ends))
        m2.append(lax.ppermute(inner, "tensor", middle))
    for p in range(PARTS):
        outer, inner = tie(m2[p], nears[p])
        e3.append(lax.ppermute(outer, "tensor", outward))
        m3.append(lax.ppermute(inner, "tensor", middle))
    for p in range(PARTS):
        m4.append(lax.ppermute(e2[p], "tensor", middle))
    far, _ = tie(far, e1[-1])

    near_rows = jnp.concatenate(
        nears
        + [jnp.where(is_end, e1[p], e2[p]) for p in range(PARTS)]
        + [jnp.where(is_end, e2[p], m1[p]) for p in range(PARTS)]
        + [jnp.where(is_end, e3[p], m2[p]) for p in range(PARTS)]
    )
    near_weight = lax.dynamic_slice_in_dim(weight, near_at, half, 0)
    far_weight = lax.dynamic_slice_in_dim(weight, far_at, half, 0)
    far_rows = jnp.concatenate([far] + e1 + m3)

    factors = pick_factors(here, all_ids, slots, order, down, up, paired, fetched)
    depth = down.shape[2]
    blocks = ids.shape[0]
    columns = lax.dynamic_slice_in_dim(near_rows, (me % 2) * depth, depth, 1)
    partial_rank = jnp.einsum(
        "bri,bki->bkr",
        columns.reshape(blocks, rows, depth),
        factors[:, :, :depth],
        preferred_element_type=jnp.float32,
    )
    back = jnp.array([[0, 1, 2, 3], [1, 0, 2, 3], [3, 2, 0, 1], [3, 2, 1, 0]], jnp.int32)[me]
    reduced = sum_over_tensor(partial_rank[back])[order].astype(jnp.bfloat16)

    near_out = dot(near_rows, near_weight)
    far_out = dot(far_rows, far_weight)
    sent = dot(jnp.concatenate([far] + m3), end_weight).astype(jnp.bfloat16)
    sent, near_out, far_out, reduced, *m4 = tie(sent, near_out, far_out, reduced, *m4)
    sent = lax.ppermute(sent, "tensor", outward)
    passed = [
        lax.ppermute(dot(rows, end_weight).astype(jnp.bfloat16), "tensor", outward) for rows in m4
    ]
    last_out = [dot(rows, far_weight) for rows in m4]
    return pl.pallas_call(
        finish_kernel,
        out_shape=jax.ShapeDtypeStruct(near_out.shape, jnp.bfloat16),
        in_specs=[SMEM] * 3 + [VMEM] * (5 + 2 * PARTS),
        out_specs=VMEM,
        compiler_params=BIG,
    )(
        order,
        live_rows,
        is_end.astype(jnp.int32)[None],
        near_out,
        far_out,
        *last_out,
        sent,
        *passed,
        reduced,
        factors,
    )


def body(
    queries,
    keys,
    values,
    lengths,
    output_projection_weight,
    adapter_down_factors,
    adapter_up_factors,
    block_adapter_index,
    block_live_rows,
    adapter_storage_slot,
):
    rows = queries.shape[0]
    replica_rows = rows * lax.axis_size("tensor")
    blocks = block_adapter_index.shape[0]
    block_rows = replica_rows // blocks
    down = jnp.swapaxes(adapter_down_factors, 1, 2)
    up = adapter_up_factors
    if lax.axis_size("tensor") == LINE and block_rows == rows:
        return line_body(
            queries,
            keys,
            values,
            lengths,
            output_projection_weight,
            down,
            up,
            block_adapter_index,
            block_live_rows,
            adapter_storage_slot,
        )
    here, all_ids, packed = pair_factors(down, up, block_adapter_index, adapter_storage_slot)
    paired, merged = merge_factors(here, all_ids, adapter_storage_slot, down, up, packed)
    fetched = fetch_factors(merged)
    attended = lax.all_gather(
        attention(queries, keys, values, lengths), "tensor", axis=0, tiled=True
    )
    order = jnp.arange(blocks, dtype=jnp.int32)
    factors = pick_factors(
        here, all_ids, adapter_storage_slot, order, down, up, paired, fetched
    )
    depth = down.shape[2]
    columns = lax.dynamic_slice_in_dim(
        attended, lax.axis_index("tensor") * depth, depth, 1
    ).reshape(blocks, block_rows, depth)
    partial_rank = jnp.einsum(
        "bri,bki->bkr", columns, factors[:, :, :depth], preferred_element_type=jnp.float32
    )
    reduced = sum_over_tensor(partial_rank).astype(jnp.bfloat16)
    base = dot(attended, output_projection_weight)
    delta = jnp.einsum(
        "bkr,bkc->brc", reduced, factors[:, :, depth:], preferred_element_type=jnp.float32
    )
    live = (jnp.arange(block_rows)[None, :] < block_live_rows[:, None])[..., None]
    base = base.reshape(delta.shape)
    return (
        jnp.where(live, base + 2.0 * delta, 0.0)
        .astype(jnp.bfloat16)
        .reshape(replica_rows, base.shape[2])
    )


def solution(mesh):
    placed = (
        P(("groups", "replica", "tensor"), None),
        P(("groups", "replica", "tensor"), None, None),
        P(("groups", "replica", "tensor"), None, None),
        P(("groups", "replica", "tensor")),
        P(None, "tensor"),
        P(("groups", "replica"), "tensor", None),
        P(("groups", "replica"), None, "tensor"),
        P(("groups", "replica")),
        P(("groups", "replica")),
        P("groups"),
    )
    return jax.shard_map(
        body,
        mesh=mesh,
        in_specs=placed,
        out_specs=P(("groups", "replica"), "tensor"),
        check_vma=False,
    )
```

time: 227 us -> 196 us (0.86)
  waiting for transfers between devices: 117 us -> 51.9 us
  starting transfers between devices: 13.5 us -> 48.9 us
  blocking collectives: 18.5 us -> 0 us
  matrix products: 30.9 us -> 44.3 us
  Pallas kernels: 0 us -> 5.59 us
  other arithmetic: 17.9 us -> 13.9 us
    all_to_all x3 -> x0, waiting for transfers between devices: 67.3 us -> none  [the longest x1 45.2 us: body(): lax.all_to_all(served_a, 'replica', split_axis=0, concat_axis=0, tiled=True)]
    ppermute x0 -> x25, waiting for transfers between devices: none -> 51.9 us  [the longest x2 15.5 us: line_body(): e3.append(lax.ppermute(outer, 'tensor', outward))]
    all_gather x1, waiting for transfers between devices: 49.9 us -> 0.02 us  [line_body(): lax.all_gather(piece, ('groups', 'replica'), axis=0, tiled=True)]
    ppermute x0 -> x25, starting transfers between devices: none -> 48.9 us  [the longest x2 15.3 us: sum_over_tensor(): lax.ppermute(partial, 'tensor', [(i, i ^ bit) for i in range(size)])]
    psum x1 -> x0, blocking collectives: 18.5 us -> none  [body(): reduced = lax.psum(partial_rank, 'tensor').astype(jnp.bfloat16)]
    all_to_all x3 -> x0, starting transfers between devices: 13.5 us -> none  [the longest x1 4.9 us: body(): lax.all_to_all(served_a, 'replica', split_axis=0, concat_axis=0, tiled=True)]
    dot_general x5 -> x10, matrix products: 30.9 us -> 44.3 us  [the longest x7 30.4 us: dot(): return jnp.dot(a, b, preferred_element_type=jnp.float32)]
    unnamed x12 -> x69, local copies, waits for them, and re-layouts: 5.41 us -> 12.1 us
  transfers between devices with their start and end apart: 4 -> 26, of which waited for: 4 -> 8; matrix products, arithmetic and copies ran while one was open for 10% -> 34% of each run, Pallas kernels for 0% -> 2%
where the time goes in v1:
time: 196 us; the launch traced here: 195 us
  waiting for transfers between devices  51.9 us (26%)
  starting transfers between devices  48.9 us (25%)
  matrix products  44.3 us (23%)
  local copies, waits for them, and re-layouts  16.5 us (8%)
  between operations  14.1 us (7%)
  other arithmetic  13.9 us (7%)
  Pallas kernels  5.59 us (3%)
    dot_general x7, matrix products, dot(): return jnp.dot(a, b, preferred_element_type=jnp.float32)  30.4 us
    ppermute x2, waiting for transfers between devices, line_body(): e3.append(lax.ppermute(outer, 'tensor', outward))  15.5 us
    ppermute x2, starting transfers between devices, sum_over_tensor(): lax.ppermute(partial, 'tensor', [(i, i ^ bit) for i in range(size)])  15.3 us
    ppermute x2, waiting for transfers between devices, line_body(): e2.append(lax.ppermute(outer, 'tensor', ends))  13.7 us
    ppermute x2, waiting for transfers between devices, line_body(): e1.append(lax.ppermute(outer, 'tensor', ends))  13.5 us
    unnamed x69, local copies, waits for them, and re-layouts  12.1 us
    dot_general x1, matrix products, attention(): jnp.einsum('rkgd,rpkd->rkgp', query_heads, key_heads, preferred_element_t...  6.96 us
    dot_general x1, matrix products, attention(): summed = jnp.einsum('rkgp,rpkd->rkgd', weights, value_heads)  6.06 us
  transfers between devices with their start and end apart: 26, of which 8 were waited for; matrix products, arithmetic and copies ran while one was open for 34% of the time, Pallas kernels for 2%

profile of v1, /device:TPU:0, one launch (start us, length us, event | category | flops | bytes accessed | tf_op | source)
XLA Modules:
  0.0 195.2 jit_solution(5725062059176902618)
XLA Ops:
  6.5 2.4 %collective-permute-start = (s32[4]{0:T(128)}, s32[4]{0:T(128)S(1)}, u32[]{:S(2)}, u32[]{:S(2)}) collective-permute-start(s32[4]{0:T(128)} %param.19), channel_id=1, source_target_pairs={{0,12},{4,0},{8,4},{12,8},{1,13},{5,1},{9,5},{13,9},{2,14},{6,2},{... | collective-permute-start | bytes 56 | tf_op jit(solution)/shard_map/ppermute | solution.py:157
  9.7 1.3 constant_dynamic-slice_fusion.4
  11.0 4.5 %collective-permute-start.12 = (bf16[512,1024]{1,0:T(8,128)(2,1)S(1)}, bf16[512,1024]{1,0:T(8,128)(2,1)}, u32[]{:S(2)}, u32[]{:S(2)}) collective-permute-start(bf16[512,1024]{1,0:T(8,128)(2,1)S(1)} %constant_dynamic-slice_fusion.4), channel_id=1, source_target_pairs={{0,1},{3,2},{4,5},{7,6},{8,9},{11,10},{12,13},{15,14},{16,17},{19,... | collective-permute-start | bytes 3145736 | tf_op jit(solution)/shard_map/ppermute | solution.py:293
  16.3 2.2 %copy.17 = bf16[16,8,64,128]{3,2,1,0:T(8,128)(2,1)S(1)} copy(bf16[16,8,64,128]{3,1,2,0:T(8,128)(2,1)} %bitcast.72) | data formatting | bytes 4194304
  18.4 7.0 %fusion.14 = (f32[128,8,8]{2,1,0:T(8,128)S(1)}, f32[128,8,8,32]{3,2,1,0:T(8,128)S(1)}) fusion(pred[128,32]{1,0:T(8,128)(4,1)S(1)} %iota_compare_fusion, bf16[128,8,8,128]{3,2,1,0:T(8,128)(2,1)S(1)} %bitcast.71, bf16[128,32,1024]{2,1,0:T(8,128)(2,1)} %param.13), kind=kOutput, calls=%fused_computation.19 | convolution fusion | flops 67887104 | bytes 11571200 | tf_op jit(solution)/shard_map/rkgd,rpkd->rkgp/dot_general | solution.py:28
  25.4 3.1 %fusion.15 = f32[128,8,8]{2,1,0:T(8,128)S(1)} fusion(f32[128,8,8,32]{3,2,1,0:T(8,128)S(1)} %get-tuple-element.69, f32[128,8,8]{2,1,0:T(8,128)S(1)} %get-tuple-element.68, pred[128,32]{1,0:T(8,128)(4,1)S(1)} %iota_compare_fusion), kind=kLoop, calls=%fused_computation.20 | loop fusion | flops 1302528 | bytes 1118208 | tf_op jit(solution)/shard_map/reduce_sum | solution.py:35
  28.6 6.1 %divide_convert_fusion = bf16[128,8,8,128]{3,2,1,0:T(8,128)(2,1)S(1)} fusion(f32[128,8,8]{2,1,0:T(8,128)S(1)} %fusion.15, f32[128,8,8,32]{3,2,1,0:T(8,128)S(1)} %get-tuple-element.69, f32[128,8,8]{2,1,0:T(8,128)S(1)} %get-tuple-element.68, pred[128,32]{1,0:T(8,128)(4,1)S(1)} %iota_compare_fusion, bf16[128,32,1024]{2,1,0:T(8,128)(2,1)} %param.14), kind=kOutput, calls=%fused_computation.16 | convolution fusion | flops 70254592 | bytes 11603968 | tf_op jit(solution)/shard_map/rkgp,rpkd->rkgd/dot_general | solution.py:36
  34.7 3.1 %copy.32 = bf16[16,8,64,128]{3,1,2,0:T(8,128)(2,1)} copy(bf16[16,8,64,128]{3,2,1,0:T(8,128)(2,1)S(1)} %bitcast.73) | data formatting | bytes 4194304
  38.8 1.6 copy-done.5
  40.5 1.1 collective-permute-start.5
  41.6 2.9 %broadcast_select_fusion.2 = (bf16[64,4096]{1,0:T(8,128)(2,1)S(1)}, bf16[64,4096]{1,0:T(8,128)(2,1)S(1)}, bf16[64,4096]{1,0:T(8,128)(2,1)S(1)}, bf16[64,4096]{1,...) fusion(pred[]{:T(512)S(6)} %or.3, bf16[128,8192]{1,0:T(8,128)(2,1)} %bitcast.68, ...), kind=kLoop, calls=%fused_computation.47 | loop fusion | flops 524288 | bytes 5242893 | tf_op jit(solution)/shard_map/jit(_where)/select_n | solution.py:307
  46.0 1.8 collective-permute-start.3
  48.5 3.2 %collective-permute-start.6 = (bf16[64,4096]{1,0:T(8,128)(2,1)S(1)}, bf16[64,4096]{1,0:T(8,128)(2,1)S(1)}, u32[]{:S(2)}, u32[]{:S(2)}) collective-permute-start(bf16[64,4096]{1,0:T(8,128)(2,1)S(1)} %get-tuple-element.35), channel_id=1, source_target_pairs={{0,1},{1,0},{2,3},{3,2},{4,5},{5,4},{6,7},{7,6},{8,9},{9,8},{10,11... | collective-permute-start | bytes 1572872 | tf_op jit(solution)/shard_map/ppermute | solution.py:308
  52.5 1.3 broadcast_select_fusion
  53.8 7.1 %collective-permute-done.3 = bf16[64,4096]{1,0:T(8,128)(2,1)S(1)} collective-permute-done((bf16[64,4096]{1,0:T(8,128)(2,1)S(1)}, bf16[64,4096]{1,0:T(8,128)(2,1)S(1)}, u32[]{:S(2)}, u32[]{:S(2)}) %collective-permute-start.3) | collective-permute-done | bytes 524320 | tf_op jit(solution)/shard_map/ppermute | solution.py:308
  60.9 1.7 collective-permute-start.14
  62.6 1.4 collective-permute-start.10
  65.7 6.4 %collective-permute-done.6 = bf16[64,4096]{1,0:T(8,128)(2,1)S(1)} collective-permute-done((bf16[64,4096]{1,0:T(8,128)(2,1)S(1)}, bf16[64,4096]{1,0:T(8,128)(2,1)S(1)}, u32[]{:S(2)}, u32[]{:S(2)}) %collective-permute-start.6) | collective-permute-done | bytes 524320 | tf_op jit(solution)/shard_map/ppermute | solution.py:308
  72.1 1.7 collective-permute-start.13
  75.9 1.4 collective-permute-start.16
  77.3 1.5 collective-permute-start.11
  78.7 4.7 %collective-permute-done.14 = bf16[64,4096]{1,0:T(8,128)(2,1)} collective-permute-done((bf16[64,4096]{1,0:T(8,128)(2,1)S(1)}, bf16[64,4096]{1,0:T(8,128)(2,1)}, u32[]{:S(2)}, u32[]{:S(2)}) %collective-permute-start.14) | collective-permute-done | bytes 524320 | tf_op jit(solution)/shard_map/ppermute | solution.py:315
  83.5 1.4 collective-permute-start.21
  85.7 9.0 %collective-permute-done.13 = bf16[64,4096]{1,0:T(8,128)(2,1)} collective-permute-done((bf16[64,4096]{1,0:T(8,128)(2,1)S(1)}, bf16[64,4096]{1,0:T(8,128)(2,1)}, u32[]{:S(2)}, u32[]{:S(2)}) %collective-permute-start.13) | collective-permute-done | bytes 524320 | tf_op jit(solution)/shard_map/ppermute | solution.py:315
  94.7 1.3 collective-permute-start.15
  97.8 1.7 select_dynamic-update-slice_fusion.3
  99.5 1.2 select_dynamic-update-slice_fusion.2
  100.7 15.5 %collective-permute-done.15 = bf16[64,4096]{1,0:T(8,128)(2,1)S(1)} collective-permute-done((bf16[64,4096]{1,0:T(8,128)(2,1)S(1)}, bf16[64,4096]{1,0:T(8,128)(2,1)S(1)}, u32[]{:S(2)}, u32[]{:S(2)}) %collective-permute-start.15) | collective-permute-done | bytes 524320 | tf_op jit(solution)/shard_map/ppermute | solution.py:319
  117.0 1.5 collective-permute-start.20
  119.6 5.9 %fusion.6.near_ref = f32[512,1024]{1,0:T(8,128)} fusion(bf16[512,4096]{1,0:T(8,128)(2,1)S(1)} %select_dynamic-update-slice_fusion, bf16[8192,1024]{1,0:T(8,128)(2,1)S(1)} %bitcast.65, s32[]{:T(128)S(6)} %select_n.106), kind=kOutput, calls=%fused_computation.8 | convolution fusion | flops 4294967296 | bytes 14680068 | tf_op jit(solution)/shard_map/dot_general | solution.py:258
  125.6 1.2 collective-permute-done.17.refs_0_
  126.8 1.6 shard_map.120.refs_6_
  129.3 1.2 copy-done.3
  131.0 12.8 %collective-permute-start.18 = (f32[4,64,128]{2,1,0:T(8,128)S(1)}, f32[4,64,128]{2,1,0:T(8,128)S(1)}, u32[]{:S(2)}, u32[]{:S(2)}) collective-permute-start(f32[4,64,128]{2,1,0:T(8,128)S(1)} %gather_fusion), channel_id=1, source_target_pairs={{0,1},{1,0},{2,3},{3,2},{4,5},{5,4},{6,7},{7,6},{8,9},{9,8},{10,11... | collective-permute-start | bytes 393224 | tf_op jit(solution)/shard_map/ppermute | solution.py:217
  143.7 1.9 constant_dynamic-update-slice_fusion
  145.6 2.2 %collective-permute-done.18 = f32[4,64,128]{2,1,0:T(8,128)S(1)} collective-permute-done((f32[4,64,128]{2,1,0:T(8,128)S(1)}, f32[4,64,128]{2,1,0:T(8,128)S(1)}, u32[]{:S(2)}, u32[]{:S(2)}) %collective-permute-start.18) | collective-permute-done | bytes 131104 | tf_op jit(solution)/shard_map/ppermute | solution.py:217
  147.8 2.6 %collective-permute-start.19 = (f32[4,64,128]{2,1,0:T(8,128)S(1)}, f32[4,64,128]{2,1,0:T(8,128)S(1)}, u32[]{:S(2)}, u32[]{:S(2)}) collective-permute-start(f32[4,64,128]{2,1,0:T(8,128)S(1)} %add.64), channel_id=1, source_target_pairs={{0,2},{1,3},{2,0},{3,1},{4,6},{5,7},{6,4},{7,5},{8,10},{9,11},{10,... | collective-permute-start | bytes 393224 | tf_op jit(solution)/shard_map/ppermute | solution.py:217
  150.4 6.8 %fusion.12.far_ref = f32[384,1024]{1,0:T(8,128)S(1)} fusion(bf16[384,4096]{1,0:T(8,128)(2,1)} %constant_dynamic-update-slice_fusion, bf16[8192,1024]{1,0:T(8,128)(2,1)} %param.16, s32[]{:T(128)S(6)} %select_n.104), kind=kOutput, calls=%fused_computation.14 | convolution fusion | flops 3221225472 | bytes 13107204 | tf_op jit(solution)/shard_map/dot_general | solution.py:258
  157.8 6.2 %fusion.27 = bf16[256,1024]{1,0:T(8,128)(2,1)S(1)} fusion(bf16[4096,1024]{1,0:T(8,128)(2,1)} %all-gather.2.cloned.1.call-done, bf16[64,4096]{1,0:T(8,128)(2,1)} %collective-permute-done.11, bf16[64,4096]{1,0:T(8,128)(2,1)} %copy-done.21, bf16[128,4096]{1,0:T(8,128)(2,1)S(1)} %copy-done.12), kind=kOutput, calls=%fused_computation.33 | convolution fusion | flops 2154037248 | bytes 11010048 | tf_op jit(solution)/shard_map/dot_general | solution.py:258
  164.1 2.8 %convolution_convert_fusion = bf16[64,1024]{1,0:T(8,128)(2,1)S(1)} fusion(bf16[64,4096]{1,0:T(8,128)(2,1)} %collective-permute-done.21, bf16[4096,1024]{1,0:T(8,128)(2,1)S(1)} %copy-done.9), kind=kOutput, calls=%fused_computation.34 | convolution fusion | flops 536936448 | bytes 9043968 | tf_op jit(solution)/shard_map/dot_general | solution.py:258
  166.9 1.6 collective-permute-start.24
  168.5 3.3 %convolution_convert_fusion.1 = bf16[64,1024]{1,0:T(8,128)(2,1)S(1)} fusion(bf16[64,4096]{1,0:T(8,128)(2,1)} %collective-permute-done.20, bf16[4096,1024]{1,0:T(8,128)(2,1)S(1)} %copy-done.9), kind=kOutput, calls=%fused_computation.35 | convolution fusion | flops 536936448 | bytes 9043968 | tf_op jit(solution)/shard_map/dot_general | solution.py:258
  171.8 1.3 collective-permute-start.23
  173.1 1.5 collective-permute-start.22
  174.6 2.6 %fusion.8.refs_1_ = f32[64,1024]{1,0:T(8,128)S(1)} fusion(bf16[64,4096]{1,0:T(8,128)(2,1)} %collective-permute-done.21, bf16[8192,1024]{1,0:T(8,128)(2,1)S(1)} %bitcast.67, s32[]{:T(128)S(6)} %select_n.104), kind=kOutput, calls=%fused_computation.10 | convolution fusion | flops 536870912 | bytes 9175044 | tf_op jit(solution)/shard_map/dot_general | solution.py:258
  177.3 2.8 %fusion.10.refs_0_ = f32[64,1024]{1,0:T(8,128)S(1)} fusion(bf16[64,4096]{1,0:T(8,128)(2,1)} %collective-permute-done.20, bf16[8192,1024]{1,0:T(8,128)(2,1)S(1)} %bitcast.67, s32[]{:T(128)S(6)} %select_n.104), kind=kOutput, calls=%fused_computation.12 | convolution fusion | flops 536870912 | bytes 9175044 | tf_op jit(solution)/shard_map/dot_general | solution.py:258
  180.2 5.9 %collective-permute-done.22.refs_2_ = bf16[256,1024]{1,0:T(8,128)(2,1)S(1)} collective-permute-done((bf16[256,1024]{1,0:T(8,128)(2,1)S(1)}, bf16[256,1024]{1,0:T(8,128)(2,1)S(1)}, u32[]{:S(2)}, u32[]{:S(2)}) %collective-permute-start.22) | collective-permute-done | bytes 524320 | tf_op jit(solution)/shard_map/ppermute | solution.py:352
  186.1 2.3 %shard_map.121 = bf16[512,1024]{1,0:T(8,128)(2,1)} custom-call(s32[4]{0:T(128)S(1)} %fusion.41.order_ref, s32[4]{0:T(128)S(1)} %copy-done.8, s32[1]{0:T(128)} %bitcast.1.end_ref, f32[512,1024]{1,0:T(8,128)S(1)} %copy-done.6, f32[384,1024]{1,0:T(8,128)S(1)} %fusion.12.far_ref, f32[64,1024]{1,0:T(8,128)S(1)} %fusion.10.refs_0_, f32[64,1024]{1,0:T(8,128)S(1)} %fusion.8.refs_1_, ...), custom_call_target="tpu_custom_call" | custom-call | tf_op jit(solution)/shard_map/pallas_call | solution.py:357
  (114 shorter events, 15.9 us)
Async XLA Ops:
  6.5 151.3 %all-gather.2.cloned.1.call-start = ((), (), s32[]{:S(2)}) async-start(), calls=%async_computation | async-start | bytes 9437184 | tf_op jit(solution)/shard_map/all_gather | solution.py:300
  6.5 31.3 %collective-permute-start = (s32[4]{0:T(128)}, s32[4]{0:T(128)S(1)}, u32[]{:S(2)}, u32[]{:S(2)}) collective-permute-start(s32[4]{0:T(128)} %param.19), channel_id=1, source_target_pairs={{0,12},{4,0},{8,4},{12,8},{1,13},{5,1},{9,5},{13,9},{2,14},{6,2},{... | collective-permute-start | bytes 56 | tf_op jit(solution)/shard_map/ppermute | solution.py:157
  8.9 28.9 %collective-permute-start.1 = (s32[4]{0:T(128)}, s32[4]{0:T(128)S(1)}, u32[]{:S(2)}, u32[]{:S(2)}) collective-permute-start(s32[4]{0:T(128)} %param.19), channel_id=1, source_target_pairs={{0,8},{4,12},{8,0},{12,4},{1,9},{5,13},{9,1},{13,5},{2,10},{6,14},... | collective-permute-start | bytes 56 | tf_op jit(solution)/shard_map/ppermute | solution.py:157
  9.5 28.3 %collective-permute-start.2 = (s32[4]{0:T(128)}, s32[4]{0:T(128)S(1)}, u32[]{:S(2)}, u32[]{:S(2)}) collective-permute-start(s32[4]{0:T(128)} %param.19), channel_id=1, source_target_pairs={{0,4},{4,8},{8,12},{12,0},{1,5},{5,9},{9,13},{13,1},{2,6},{6,10},{... | collective-permute-start | bytes 56 | tf_op jit(solution)/shard_map/ppermute | solution.py:157
  11.0 29.5 %collective-permute-start.12 = (bf16[512,1024]{1,0:T(8,128)(2,1)S(1)}, bf16[512,1024]{1,0:T(8,128)(2,1)}, u32[]{:S(2)}, u32[]{:S(2)}) collective-permute-start(bf16[512,1024]{1,0:T(8,128)(2,1)S(1)} %constant_dynamic-slice_fusion.4), channel_id=1, source_target_pairs={{0,1},{3,2},{4,5},{7,6},{8,9},{11,10},{12,13},{15,14},{16,17},{19,... | collective-permute-start | bytes 3145736 | tf_op jit(solution)/shard_map/ppermute | solution.py:293
  28.5 9.3 %copy-start.1 = (bf16[12,64,1024]{2,1,0:T(8,128)(2,1)S(1)}, bf16[12,64,1024]{2,1,0:T(8,128)(2,1)}, u32[]{:S(2)}) copy-start(bf16[12,64,1024]{2,1,0:T(8,128)(2,1)} %up_ref.5) | copy-start | bytes 4718596
  40.5 23.5 %collective-permute-start.5 = (bf16[2,4,64,3072]{3,2,1,0:T(8,128)(2,1)}, bf16[2,4,64,3072]{3,2,1,0:T(8,128)(2,1)}, u32[]{:S(2)}, u32[]{:S(2)}) collective-permute-start(bf16[2,4,64,3072]{3,2,1,0:T(8,128)(2,1)} %copy-done.5), channel_id=1, source_target_pairs={{0,4},{4,0},{8,12},{12,8},{1,5},{5,1},{9,13},{13,9},{2,6},{6,2},{1... | collective-permute-start | bytes 9437192 | tf_op jit(solution)/shard_map/ppermute | solution.py:177
  41.6 22.4 %copy-start.2 = (bf16[12,64,1024]{2,1,0:T(8,128)(2,1)S(1)}, bf16[12,64,1024]{2,1,0:T(8,128)(2,1)}, u32[]{:S(2)}) copy-start(bf16[12,64,1024]{2,1,0:T(8,128)(2,1)} %up_ref.5) | copy-start | bytes 4718596
  44.6 20.3 %copy-start.13 = (bf16[64,4096]{1,0:T(8,128)(2,1)}, bf16[64,4096]{1,0:T(8,128)(2,1)S(1)}, u32[]{:S(2)}) copy-start(bf16[64,4096]{1,0:T(8,128)(2,1)S(1)} %get-tuple-element.37) | copy-start | bytes 1572868
  44.6 7.1 %collective-permute-start.9 = (bf16[64,4096]{1,0:T(8,128)(2,1)S(1)}, bf16[64,4096]{1,0:T(8,128)(2,1)S(1)}, u32[]{:S(2)}, u32[]{:S(2)}) collective-permute-start(bf16[64,4096]{1,0:T(8,128)(2,1)S(1)} %get-tuple-element.38), channel_id=1, source_target_pairs={{1,2},{2,1},{5,6},{6,5},{9,10},{10,9},{13,14},{14,13},{17,18},{18,... | collective-permute-start | bytes 1572872 | tf_op jit(solution)/shard_map/ppermute | solution.py:309
  46.0 14.8 %collective-permute-start.3 = (bf16[64,4096]{1,0:T(8,128)(2,1)S(1)}, bf16[64,4096]{1,0:T(8,128)(2,1)S(1)}, u32[]{:S(2)}, u32[]{:S(2)}) collective-permute-start(bf16[64,4096]{1,0:T(8,128)(2,1)S(1)} %get-tuple-element.30), channel_id=1, source_target_pairs={{0,1},{1,0},{2,3},{3,2},{4,5},{5,4},{6,7},{7,6},{8,9},{9,8},{10,11... | collective-permute-start | bytes 1572872 | tf_op jit(solution)/shard_map/ppermute | solution.py:308
  47.8 17.0 %collective-permute-start.4 = (bf16[64,4096]{1,0:T(8,128)(2,1)S(1)}, bf16[64,4096]{1,0:T(8,128)(2,1)S(1)}, u32[]{:S(2)}, u32[]{:S(2)}) collective-permute-start(bf16[64,4096]{1,0:T(8,128)(2,1)S(1)} %get-tuple-element.32), channel_id=1, source_target_pairs={{1,2},{2,1},{5,6},{6,5},{9,10},{10,9},{13,14},{14,13},{17,18},{18,... | collective-permute-start | bytes 1572872 | tf_op jit(solution)/shard_map/ppermute | solution.py:309
  48.5 23.6 %collective-permute-start.6 = (bf16[64,4096]{1,0:T(8,128)(2,1)S(1)}, bf16[64,4096]{1,0:T(8,128)(2,1)S(1)}, u32[]{:S(2)}, u32[]{:S(2)}) collective-permute-start(bf16[64,4096]{1,0:T(8,128)(2,1)S(1)} %get-tuple-element.35), channel_id=1, source_target_pairs={{0,1},{1,0},{2,3},{3,2},{4,5},{5,4},{6,7},{7,6},{8,9},{9,8},{10,11... | collective-permute-start | bytes 1572872 | tf_op jit(solution)/shard_map/ppermute | solution.py:308
  52.5 67.1 %slice-start = ((s8[16777216]{0:T(1024)(128)(4,1)}), s8[4194304]{0:T(1024)(128)(4,1)S(1)}, s32[]{:S(2)}) async-start(s8[16777216]{0:T(1024)(128)(4,1)} %bitcast.64), calls=%async_computation.1 | async-start | bytes 8388608
  53.8 20.7 %copy-start.10 = (bf16[16,8,64,128]{3,1,2,0:T(8,128)(2,1)S(1)}, bf16[16,8,64,128]{3,1,2,0:T(8,128)(2,1)}, u32[]{:S(2)}) copy-start(bf16[16,8,64,128]{3,1,2,0:T(8,128)(2,1)} %copy.32) | copy-start | bytes 6291460
  53.8 65.8 %slice-start.1 = ((s8[16777216]{0:T(1024)(128)(4,1)}), s8[4194304]{0:T(1024)(128)(4,1)S(1)}, s32[]{:S(2)}) async-start(s8[16777216]{0:T(1024)(128)(4,1)} %bitcast.64), calls=%async_computation.2 | async-start | bytes 8388608
  60.9 22.6 %collective-permute-start.14 = (bf16[64,4096]{1,0:T(8,128)(2,1)S(1)}, bf16[64,4096]{1,0:T(8,128)(2,1)}, u32[]{:S(2)}, u32[]{:S(2)}) collective-permute-start(bf16[64,4096]{1,0:T(8,128)(2,1)S(1)} %broadcast_select_fusion), channel_id=1, source_target_pairs={{0,1},{1,0},{2,3},{3,2},{4,5},{5,4},{6,7},{7,6},{8,9},{9,8},{10,11... | collective-permute-start | bytes 1572872 | tf_op jit(solution)/shard_map/ppermute | solution.py:315
  62.6 13.3 %collective-permute-start.10 = (bf16[64,4096]{1,0:T(8,128)(2,1)S(1)}, bf16[64,4096]{1,0:T(8,128)(2,1)}, u32[]{:S(2)}, u32[]{:S(2)}) collective-permute-start(bf16[64,4096]{1,0:T(8,128)(2,1)S(1)} %collective-permute-done.3), channel_id=1, source_target_pairs={{1,2},{2,1},{5,6},{6,5},{9,10},{10,9},{13,14},{14,13},{17,18},{18,... | collective-permute-start | bytes 1572872 | tf_op jit(solution)/shard_map/ppermute | solution.py:316
  65.7 31.2 %copy-start.20 = (bf16[64,4096]{1,0:T(8,128)(2,1)S(1)}, bf16[64,4096]{1,0:T(8,128)(2,1)}, u32[]{:S(2)}) copy-start(bf16[64,4096]{1,0:T(8,128)(2,1)} %copy-done.19) | copy-start | bytes 1572868
  65.7 53.9 %slice-start.2 = ((s8[16777216]{0:T(1024)(128)(4,1)}), s8[4194304]{0:T(1024)(128)(4,1)S(1)}, s32[]{:S(2)}) async-start(s8[16777216]{0:T(1024)(128)(4,1)} %bitcast.64), calls=%async_computation.3 | async-start | bytes 8388608
  72.1 22.6 %collective-permute-start.13 = (bf16[64,4096]{1,0:T(8,128)(2,1)S(1)}, bf16[64,4096]{1,0:T(8,128)(2,1)}, u32[]{:S(2)}, u32[]{:S(2)}) collective-permute-start(bf16[64,4096]{1,0:T(8,128)(2,1)S(1)} %broadcast_select_fusion.1), channel_id=1, source_target_pairs={{0,1},{1,0},{2,3},{3,2},{4,5},{5,4},{6,7},{7,6},{8,9},{9,8},{10,11... | collective-permute-start | bytes 1572872 | tf_op jit(solution)/shard_map/ppermute | solution.py:315
  73.8 11.1 %collective-permute-start.7 = (bf16[64,4096]{1,0:T(8,128)(2,1)S(1)}, bf16[64,4096]{1,0:T(8,128)(2,1)S(1)}, u32[]{:S(2)}, u32[]{:S(2)}) collective-permute-start(bf16[64,4096]{1,0:T(8,128)(2,1)S(1)} %collective-permute-done.6), channel_id=1, source_target_pairs={{1,2},{2,1},{5,6},{6,5},{9,10},{10,9},{13,14},{14,13},{17,18},{18,... | collective-permute-start | bytes 1572872 | tf_op jit(solution)/shard_map/ppermute | solution.py:316
  74.7 10.2 %copy-start.11 = (bf16[128,4096]{1,0:T(8,128)(2,1)}, bf16[128,4096]{1,0:T(8,128)(2,1)S(1)}, u32[]{:S(2)}) copy-start(bf16[128,4096]{1,0:T(8,128)(2,1)S(1)} %get-tuple-element.31) | copy-start | bytes 3145732
  74.7 23.1 %copy-start.18 = (bf16[64,4096]{1,0:T(8,128)(2,1)S(1)}, bf16[64,4096]{1,0:T(8,128)(2,1)}, u32[]{:S(2)}) copy-start(bf16[64,4096]{1,0:T(8,128)(2,1)} %copy-done.17) | copy-start | bytes 1572868
  74.7 24.8 %copy-start.16 = (bf16[64,4096]{1,0:T(8,128)(2,1)S(1)}, bf16[64,4096]{1,0:T(8,128)(2,1)}, u32[]{:S(2)}) copy-start(bf16[64,4096]{1,0:T(8,128)(2,1)} %copy-done.15) | copy-start | bytes 1572868
  75.9 40.3 %copy-start.14 = (bf16[64,4096]{1,0:T(8,128)(2,1)S(1)}, bf16[64,4096]{1,0:T(8,128)(2,1)}, u32[]{:S(2)}) copy-start(bf16[64,4096]{1,0:T(8,128)(2,1)} %copy-done.13) | copy-start | bytes 1572868
  75.9 41.1 %collective-permute-start.16 = (bf16[64,4096]{1,0:T(8,128)(2,1)}, bf16[64,4096]{1,0:T(8,128)(2,1)S(1)}, u32[]{:S(2)}, u32[]{:S(2)}) collective-permute-start(bf16[64,4096]{1,0:T(8,128)(2,1)} %collective-permute-done.10), channel_id=1, source_target_pairs={{1,0},{2,3},{5,4},{6,7},{9,8},{10,11},{13,12},{14,15},{17,16},{18,... | collective-permute-start | bytes 1572872 | tf_op jit(solution)/shard_map/ppermute | solution.py:319
  77.3 66.5 %collective-permute-start.11 = (bf16[64,4096]{1,0:T(8,128)(2,1)}, bf16[64,4096]{1,0:T(8,128)(2,1)}, u32[]{:S(2)}, u32[]{:S(2)}) collective-permute-start(bf16[64,4096]{1,0:T(8,128)(2,1)} %get-tuple-element.40), channel_id=1, source_target_pairs={{1,2},{2,1},{5,6},{6,5},{9,10},{10,9},{13,14},{14,13},{17,18},{18,... | collective-permute-start | bytes 1572872 | tf_op jit(solution)/shard_map/ppermute | solution.py:320
  83.5 80.6 %collective-permute-start.21 = (bf16[64,4096]{1,0:T(8,128)(2,1)}, bf16[64,4096]{1,0:T(8,128)(2,1)}, u32[]{:S(2)}, u32[]{:S(2)}) collective-permute-start(bf16[64,4096]{1,0:T(8,128)(2,1)} %collective-permute-done.14), channel_id=1, source_target_pairs={{1,2},{2,1},{5,6},{6,5},{9,10},{10,9},{13,14},{14,13},{17,18},{18,... | collective-permute-start | bytes 1572872 | tf_op jit(solution)/shard_map/ppermute | solution.py:322
  84.9 41.9 %collective-permute-start.17 = (bf16[4,64,3072]{2,1,0:T(8,128)(2,1)S(1)}, bf16[4,64,3072]{2,1,0:T(8,128)(2,1)S(1)}, u32[]{:S(2)}, u32[]{:S(2)}) collective-permute-start(bf16[4,64,3072]{2,1,0:T(8,128)(2,1)S(1)} %bitcast.63), channel_id=1, source_target_pairs={{0,8},{4,12},{8,0},{12,4},{1,9},{5,13},{9,1},{13,5},{2,10},{6,14},... | collective-permute-start | bytes 4718600 | tf_op jit(solution)/shard_map/ppermute | solution.py:192
  94.7 21.5 %collective-permute-start.15 = (bf16[64,4096]{1,0:T(8,128)(2,1)S(1)}, bf16[64,4096]{1,0:T(8,128)(2,1)S(1)}, u32[]{:S(2)}, u32[]{:S(2)}) collective-permute-start(bf16[64,4096]{1,0:T(8,128)(2,1)S(1)} %collective-permute-done.7), channel_id=1, source_target_pairs={{1,0},{2,3},{5,4},{6,7},{9,8},{10,11},{13,12},{14,15},{17,16},{18,... | collective-permute-start | bytes 1572872 | tf_op jit(solution)/shard_map/ppermute | solution.py:319
  96.9 22.6 %slice-start.3 = ((s8[16777216]{0:T(1024)(128)(4,1)}), s8[4194304]{0:T(1024)(128)(4,1)S(1)}, s32[]{:S(2)}) async-start(s8[16777216]{0:T(1024)(128)(4,1)} %bitcast.64), calls=%async_computation.4 | async-start | bytes 8388608
  116.2 2.5 %collective-permute-start.8 = (bf16[64,4096]{1,0:T(8,128)(2,1)S(1)}, bf16[64,4096]{1,0:T(8,128)(2,1)S(1)}, u32[]{:S(2)}, u32[]{:S(2)}) collective-permute-start(bf16[64,4096]{1,0:T(8,128)(2,1)S(1)} %copy-done.14), channel_id=1, source_target_pairs={{1,2},{2,1},{5,6},{6,5},{9,10},{10,9},{13,14},{14,13},{17,18},{18,... | collective-permute-start | bytes 1572872 | tf_op jit(solution)/shard_map/ppermute | solution.py:320
  117.0 47.0 %collective-permute-start.20 = (bf16[64,4096]{1,0:T(8,128)(2,1)}, bf16[64,4096]{1,0:T(8,128)(2,1)}, u32[]{:S(2)}, u32[]{:S(2)}) collective-permute-start(bf16[64,4096]{1,0:T(8,128)(2,1)} %collective-permute-done.13), channel_id=1, source_target_pairs={{1,2},{2,1},{5,6},{6,5},{9,10},{10,9},{13,14},{14,13},{17,18},{18,... | collective-permute-start | bytes 1572872 | tf_op jit(solution)/shard_map/ppermute | solution.py:322
  118.6 6.9 %copy-start.21 = (bf16[64,4096]{1,0:T(8,128)(2,1)}, bf16[64,4096]{1,0:T(8,128)(2,1)S(1)}, u32[]{:S(2)}) copy-start(bf16[64,4096]{1,0:T(8,128)(2,1)S(1)} %collective-permute-done.8) | copy-start | bytes 1572868
  131.0 16.8 %collective-permute-start.18 = (f32[4,64,128]{2,1,0:T(8,128)S(1)}, f32[4,64,128]{2,1,0:T(8,128)S(1)}, u32[]{:S(2)}, u32[]{:S(2)}) collective-permute-start(f32[4,64,128]{2,1,0:T(8,128)S(1)} %gather_fusion), channel_id=1, source_target_pairs={{0,1},{1,0},{2,3},{3,2},{4,5},{5,4},{6,7},{7,6},{8,9},{9,8},{10,11... | collective-permute-start | bytes 393224 | tf_op jit(solution)/shard_map/ppermute | solution.py:217
  147.8 10.0 %copy-start.12 = (bf16[128,4096]{1,0:T(8,128)(2,1)S(1)}, bf16[128,4096]{1,0:T(8,128)(2,1)}, u32[]{:S(2)}) copy-start(bf16[128,4096]{1,0:T(8,128)(2,1)} %copy-done.11) | copy-start | bytes 3145732
  147.8 9.4 %collective-permute-start.19 = (f32[4,64,128]{2,1,0:T(8,128)S(1)}, f32[4,64,128]{2,1,0:T(8,128)S(1)}, u32[]{:S(2)}, u32[]{:S(2)}) collective-permute-start(f32[4,64,128]{2,1,0:T(8,128)S(1)} %add.64), channel_id=1, source_target_pairs={{0,2},{1,3},{2,0},{3,1},{4,6},{5,7},{6,4},{7,5},{8,10},{9,11},{10,... | collective-permute-start | bytes 393224 | tf_op jit(solution)/shard_map/ppermute | solution.py:217
  164.0 10.6 %slice-start.4 = ((s8[16777216]{0:T(1024)(128)(4,1)}), s8[4194304]{0:T(1024)(128)(4,1)S(1)}, s32[]{:S(2)}) async-start(s8[16777216]{0:T(1024)(128)(4,1)} %bitcast.66), calls=%async_computation.5 | async-start | bytes 8388608
  164.1 10.6 %slice-start.5 = ((s8[16777216]{0:T(1024)(128)(4,1)}), s8[4194304]{0:T(1024)(128)(4,1)S(1)}, s32[]{:S(2)}) async-start(s8[16777216]{0:T(1024)(128)(4,1)} %bitcast.66), calls=%async_computation.6 | async-start | bytes 8388608
  166.9 7.7 %slice-start.6 = ((s8[16777216]{0:T(1024)(128)(4,1)}), s8[4194304]{0:T(1024)(128)(4,1)S(1)}, s32[]{:S(2)}) async-start(s8[16777216]{0:T(1024)(128)(4,1)} %bitcast.66), calls=%async_computation.7 | async-start | bytes 8388608
  166.9 7.7 %slice-start.7 = ((s8[16777216]{0:T(1024)(128)(4,1)}), s8[4194304]{0:T(1024)(128)(4,1)S(1)}, s32[]{:S(2)}) async-start(s8[16777216]{0:T(1024)(128)(4,1)} %bitcast.66), calls=%async_computation.8 | async-start | bytes 8388608
  166.9 13.2 %collective-permute-start.24 = (bf16[64,1024]{1,0:T(8,128)(2,1)S(1)}, bf16[64,1024]{1,0:T(8,128)(2,1)S(1)}, u32[]{:S(2)}, u32[]{:S(2)}) collective-permute-start(bf16[64,1024]{1,0:T(8,128)(2,1)S(1)} %convolution_convert_fusion), channel_id=1, source_target_pairs={{1,0},{2,3},{5,4},{6,7},{9,8},{10,11},{13,12},{14,15},{17,16},{18,... | collective-permute-start | bytes 393224 | tf_op jit(solution)/shard_map/ppermute | solution.py:354
  171.8 8.4 %collective-permute-start.23 = (bf16[64,1024]{1,0:T(8,128)(2,1)S(1)}, bf16[64,1024]{1,0:T(8,128)(2,1)S(1)}, u32[]{:S(2)}, u32[]{:S(2)}) collective-permute-start(bf16[64,1024]{1,0:T(8,128)(2,1)S(1)} %convolution_convert_fusion.1), channel_id=1, source_target_pairs={{1,0},{2,3},{5,4},{6,7},{9,8},{10,11},{13,12},{14,15},{17,16},{18,... | collective-permute-start | bytes 393224 | tf_op jit(solution)/shard_map/ppermute | solution.py:354
  173.1 13.0 %collective-permute-start.22 = (bf16[256,1024]{1,0:T(8,128)(2,1)S(1)}, bf16[256,1024]{1,0:T(8,128)(2,1)S(1)}, u32[]{:S(2)}, u32[]{:S(2)}) collective-permute-start(bf16[256,1024]{1,0:T(8,128)(2,1)S(1)} %fusion.27), channel_id=1, source_target_pairs={{1,0},{2,3},{5,4},{6,7},{9,8},{10,11},{13,12},{14,15},{17,16},{18,... | collective-permute-start | bytes 1572872 | tf_op jit(solution)/shard_map/ppermute | solution.py:352
  177.3 8.7 %copy-start.4 = (bf16[4,64,3072]{2,1,0:T(8,128)(2,1)S(1)}, bf16[4,64,3072]{2,1,0:T(8,128)(2,1)}, u32[]{:S(2)}) copy-start(bf16[4,64,3072]{2,1,0:T(8,128)(2,1)} %copy-done.3) | copy-start | bytes 4718596
  177.3 8.7 %copy-start.6 = (f32[512,1024]{1,0:T(8,128)S(1)}, f32[512,1024]{1,0:T(8,128)}, u32[]{:S(2)}) copy-start(f32[512,1024]{1,0:T(8,128)} %fusion.6.near_ref) | copy-start | bytes 6291460
  177.3 8.7 %copy-start.8 = (s32[4]{0:T(128)S(1)}, s32[4]{0:T(128)}, u32[]{:S(2)}) copy-start(s32[4]{0:T(128)} %live_ref.1) | copy-start | bytes 52
  (10 other events, 29.0 us)
Sparse Core Ops, SparseCore 0:
  40.6 60.6 all-gather.1

commit v2 on v1

--- a/solution.py
+++ b/solution.py
@@ -83,11 +83,12 @@
 
     def each(act):
         for k in range(1, pairs):
-            target = lax.rem(pair + k, pairs) * 2 + core
+            to = lax.rem(pair + k, pairs)
+            target = to * 2 + core
             for b in range(blocks):
                 slot = slot_of(replicas, ids_ref, slots_ref, here, target, b)
                 home = lax.div(slot, own)
-                place = out_ref.at[k - 1, b]
+                place = out_ref.at[to, b]
 
                 @pl.when(home == here)
                 def _():
@@ -113,10 +114,10 @@
     down_ref,
     up_ref,
     paired_ref,
-    *refs,
+    fetched_ref,
+    out_ref,
+    sems,
 ):
-    out_ref, sems = refs[-2:]
-    fetched = refs[:-2]
     own = down_ref.shape[0]
     pairs = replicas // 2
     here = here_ref[0]
@@ -137,11 +138,13 @@
             def _():
                 act(pltpu.make_async_copy(paired_ref.at[0, b], out_ref.at[i], sems.at[i, 0]))
 
-            for k in range(1, pairs):
-
-                @pl.when(shift == k)
-                def _():
-                    act(pltpu.make_async_copy(fetched[k - 1].at[b], out_ref.at[i], sems.at[i, 0]))
+            @pl.when(shift != 0)
+            def _():
+                act(
+                    pltpu.make_async_copy(
+                        fetched_ref.at[lax.div(home, 2), b], out_ref.at[i], sems.at[i, 0]
+                    )
+                )
 
     each(lambda copy: copy.start())
     each(lambda copy: copy.wait())
@@ -177,7 +180,7 @@
     paired = lax.ppermute(packed, "replica", [(i, i ^ 1) for i in range(replicas)])
     merged = pl.pallas_call(
         functools.partial(merge_kernel, replicas, blocks),
-        out_shape=jax.ShapeDtypeStruct((pairs - 1,) + packed.shape[1:], down.dtype),
+        out_shape=jax.ShapeDtypeStruct(packed.shape, down.dtype),
         in_specs=[SMEM] * 3 + [ANY] * 3,
         out_specs=VMEM,
         scratch_shapes=[pltpu.SemaphoreType.DMA((pairs - 1, blocks, 2))],
@@ -188,12 +191,10 @@
 
 def fetch_factors(merged):
     replicas = lax.axis_size("replica")
-    return [
-        lax.ppermute(
-            merged[k - 1], "replica", [(i, (i + 2 * k) % replicas) for i in range(replicas)]
-        )
-        for k in range(1, replicas // 2)
-    ]
+    groups = [list(range(core, replicas, 2)) for core in range(2)]
+    return lax.all_to_all(
+        merged, "replica", split_axis=0, concat_axis=0, tiled=True, axis_index_groups=groups
+    )
 
 
 def pick_factors(here, all_ids, slots, order, down, up, paired, fetched):
@@ -202,11 +203,11 @@
     return pl.pallas_call(
         functools.partial(pick_kernel, replicas, blocks),
         out_shape=jax.ShapeDtypeStruct(paired.shape[1:], down.dtype),
-        in_specs=[SMEM] * 4 + [ANY] * (3 + len(fetched)),
+        in_specs=[SMEM] * 4 + [ANY] * 4,
         out_specs=VMEM,
         scratch_shapes=[pltpu.SemaphoreType.DMA((blocks, 2))],
         compiler_params=BIG,
-    )(here, all_ids, slots, order, down, up, paired, *fetched)
+    )(here, all_ids, slots, order, down, up, paired, fetched)
 
 
 def sum_over_tensor(partial):
@@ -220,11 +221,9 @@
     return partial
 
 
-def finish_kernel(order_ref, live_ref, end_ref, near_ref, far_ref, *refs):
-    lasts = refs[:PARTS]
-    sent_ref = refs[PARTS]
-    passed_lasts = refs[PARTS + 1 : 2 * PARTS + 1]
-    reduced_ref, factors_ref, result_ref = refs[2 * PARTS + 1 :]
+def finish_kernel(order_ref, live_ref, end_ref, near_ref, early_ref, late_ref, *refs):
+    passed_refs = refs[:3]
+    reduced_ref, factors_ref, result_ref = refs[3:]
     blocks = reduced_ref.shape[0]
     rows = near_ref.shape[0] // blocks
     depth = factors_ref.shape[2] - near_ref.shape[1]
@@ -237,16 +236,10 @@
             (((0,), (0,)), ((), ())),
             preferred_element_type=jnp.float32,
         )
-        if i < 3:
-            other = far_ref[pl.ds(i * rows, rows), :]
-        else:
-            other = jnp.concatenate([ref[...] for ref in lasts])
+        other_ref = early_ref if i < 2 else late_ref
+        other = other_ref[pl.ds(i % 2 * rows, rows), :]
         if i > 0:
-            if i < 3:
-                passed = sent_ref[pl.ds((i - 1) * rows, rows), :]
-            else:
-                passed = jnp.concatenate([ref[...] for ref in passed_lasts])
-            other = jnp.where(at_end, passed.astype(jnp.float32), other)
+            other = jnp.where(at_end, passed_refs[i - 1][...].astype(jnp.float32), other)
         total = near_ref[pl.ds(i * rows, rows), :] + other + 2.0 * delta
         live = lax.broadcasted_iota(jnp.int32, total.shape, 0) < live_ref[b]
         result_ref[pl.ds(pl.multiple_of(b * rows, rows), rows), :] = jnp.where(
@@ -302,7 +295,7 @@
     far = lax.dynamic_slice_in_dim(attended, far_at, half, 1)
     nears = [near[p * cut : (p + 1) * cut] for p in range(PARTS)]
     fars = [far[p * cut : (p + 1) * cut] for p in range(PARTS)]
-    e1, e2, e3, m1, m2, m3, m4 = ([] for _ in range(7))
+    e1, e2, m1, m2 = ([] for _ in range(4))
     for p in range(PARTS):
         outer, inner = tie(jnp.where(is_end, fars[p], nears[p]), fars[p])
         e1.append(lax.ppermute(outer, "tensor", ends))
@@ -314,13 +307,16 @@
         outer, inner = tie(jnp.where(is_end, nears[p], m1[p]), e1[p])
         e2.append(lax.ppermute(outer, "tensor", ends))
         m2.append(lax.ppermute(inner, "tensor", middle))
+    far_half = lax.dynamic_slice_in_dim(weight, far_at, half, 0)
+    far, _ = tie(far, e1[-1])
+    early_out = dot(jnp.concatenate([far] + e1), far_half)
+    e2[-1], early_out = tie(e2[-1], early_out)
+    m3, m4, e3 = [], [], []
     for p in range(PARTS):
-        outer, inner = tie(m2[p], nears[p])
-        e3.append(lax.ppermute(outer, "tensor", outward))
+        inner, *_ = tie(nears[p], *m2)
+        e3.append(lax.ppermute(m2[p], "tensor", outward))
         m3.append(lax.ppermute(inner, "tensor", middle))
-    for p in range(PARTS):
         m4.append(lax.ppermute(e2[p], "tensor", middle))
-    far, _ = tie(far, e1[-1])
 
     near_rows = jnp.concatenate(
         nears
@@ -329,10 +325,9 @@
         + [jnp.where(is_end, e3[p], m2[p]) for p in range(PARTS)]
     )
     near_weight = lax.dynamic_slice_in_dim(weight, near_at, half, 0)
-    far_weight = lax.dynamic_slice_in_dim(weight, far_at, half, 0)
-    far_rows = jnp.concatenate([far] + e1 + m3)
-
-    factors = pick_factors(here, all_ids, slots, order, down, up, paired, fetched)
+
+    pick_order, *_ = tie(order, *e3)
+    factors = pick_factors(here, all_ids, slots, pick_order, down, up, paired, fetched)
     depth = down.shape[2]
     blocks = ids.shape[0]
     columns = lax.dynamic_slice_in_dim(near_rows, (me % 2) * depth, depth, 1)
@@ -346,18 +341,20 @@
     reduced = sum_over_tensor(partial_rank[back])[order].astype(jnp.bfloat16)
 
     near_out = dot(near_rows, near_weight)
-    far_out = dot(far_rows, far_weight)
-    sent = dot(jnp.concatenate([far] + m3), end_weight).astype(jnp.bfloat16)
-    sent, near_out, far_out, reduced, *m4 = tie(sent, near_out, far_out, reduced, *m4)
-    sent = lax.ppermute(sent, "tensor", outward)
-    passed = [
-        lax.ppermute(dot(rows, end_weight).astype(jnp.bfloat16), "tensor", outward) for rows in m4
-    ]
-    last_out = [dot(rows, far_weight) for rows in m4]
+    near_out, _ = tie(near_out, partial_rank)
+    inner = jnp.concatenate(m3)
+    inner_sent = dot(jnp.concatenate([far, inner]), end_weight).astype(jnp.bfloat16)
+    inner_passed = lax.ppermute(inner_sent, "tensor", outward)
+    inner_sent, near_out, reduced, *m4 = tie(inner_sent, near_out, reduced, *m4)
+    last = jnp.concatenate(m4)
+    last_sent = dot(last, end_weight).astype(jnp.bfloat16)
+    last_passed = lax.ppermute(last_sent, "tensor", outward)
+    inner, _ = tie(inner, last_sent)
+    late_out = dot(jnp.concatenate([inner, last]), far_half)
     return pl.pallas_call(
         finish_kernel,
         out_shape=jax.ShapeDtypeStruct(near_out.shape, jnp.bfloat16),
-        in_specs=[SMEM] * 3 + [VMEM] * (5 + 2 * PARTS),
+        in_specs=[SMEM] * 3 + [VMEM] * 8,
         out_specs=VMEM,
         compiler_params=BIG,
     )(
@@ -365,10 +362,11 @@
         live_rows,
         is_end.astype(jnp.int32)[None],
         near_out,
-        far_out,
-        *last_out,
-        sent,
-        *passed,
+        early_out,
+        late_out,
+        inner_passed[:rows],
+        inner_passed[rows:],
+        last_passed,
         reduced,
         factors,
     )

time: 196 us -> 186 us (0.949)
  waiting for transfers between devices: 51.9 us -> 39.4 us
  other arithmetic: 13.9 us -> 20.7 us
  starting transfers between devices: 48.9 us -> 44.4 us
    ppermute x2, waiting for transfers between devices: 13.7 us -> 0.01 us  [line_body(): e2.append(lax.ppermute(outer, 'tensor', ends))]
    ppermute x2, starting transfers between devices: 15.3 us -> 4.03 us  [sum_over_tensor(): lax.ppermute(partial, 'tensor', [(i, i ^ bit) for i in range(size)])]
    all_to_all x0 -> x1, starting transfers between devices: none -> 5.2 us  [fetch_factors(): lax.all_to_all(merged, 'replica', split_axis=0, concat_axis=0, tiled=True...]
    ppermute x6 -> x4, waiting for transfers between devices: 22.5 us -> 18.2 us  [the longest x2 10.8 us: line_body(): e3.append(lax.ppermute(m2[p], 'tensor', outward))]
    all_to_all x0 -> x1, waiting for transfers between devices: none -> 4 us  [fetch_factors(): lax.all_to_all(merged, 'replica', split_axis=0, concat_axis=0, tiled=True...]
    unnamed x7 -> x6, other arithmetic: 4.85 us -> 8.84 us
    dynamic_slice x1, local copies, waits for them, and re-layouts: 0.14 us -> 3.17 us  [line_body(): columns = lax.dynamic_slice_in_dim(near_rows, me % 2 * depth, depth, 1)]
    concatenate x0 -> x1, other arithmetic: none -> 2.26 us  [line_body(): inner = jnp.concatenate(m3)]
  transfers between devices with their start and end apart: 26 -> 25, of which waited for: 8 -> 7; matrix products, arithmetic and copies ran while one was open for 34% -> 41% of each run, Pallas kernels for 2% -> 3%
where the time goes in v2:
time: 186 us; the launch traced here: 185 us
  starting transfers between devices  44.4 us (24%)
  matrix products  42.6 us (23%)
  waiting for transfers between devices  39.4 us (21%)
  other arithmetic  20.7 us (11%)
  local copies, waits for them, and re-layouts  16.5 us (9%)
  between operations  14 us (8%)
  Pallas kernels  7.02 us (4%)
    dot_general x5, matrix products, dot(): return jnp.dot(a, b, preferred_element_type=jnp.float32)  28.8 us
    ppermute x2, waiting for transfers between devices, line_body(): e1.append(lax.ppermute(outer, 'tensor', ends))  13.5 us
    ppermute x2, waiting for transfers between devices, line_body(): e3.append(lax.ppermute(m2[p], 'tensor', outward))  10.8 us
    unnamed x59, local copies, waits for them, and re-layouts  10.8 us
    unnamed x6, other arithmetic  8.84 us
    dot_general x1, matrix products, attention(): jnp.einsum('rkgd,rpkd->rkgp', query_heads, key_heads, preferred_element_t...  6.96 us
    dot_general x1, matrix products, attention(): summed = jnp.einsum('rkgp,rpkd->rkgd', weights, value_heads)  5.99 us
    ppermute x2, starting transfers between devices, line_body(): e2.append(lax.ppermute(outer, 'tensor', ends))  5.39 us
  transfers between devices with their start and end apart: 25, of which 7 were waited for; matrix products, arithmetic and copies ran while one was open for 41% of the time, Pallas kernels for 3%

profile of v2, /device:TPU:0, one launch (start us, length us, event | category | flops | bytes accessed | tf_op | source)
XLA Modules:
  0.0 184.6 jit_solution(2214886682473231559)
XLA Ops:
  6.5 2.4 %collective-permute-start = (s32[4]{0:T(128)}, s32[4]{0:T(128)S(1)}, u32[]{:S(2)}, u32[]{:S(2)}) collective-permute-start(s32[4]{0:T(128)} %param.19), channel_id=1, source_target_pairs={{0,12},{4,0},{8,4},{12,8},{1,13},{5,1},{9,5},{13,9},{2,14},{6,2},{... | collective-permute-start | bytes 56 | tf_op jit(solution)/shard_map/ppermute | solution.py:160
  9.7 1.3 constant_dynamic-slice_fusion.4
  11.0 4.5 %collective-permute-start.12 = (bf16[512,1024]{1,0:T(8,128)(2,1)S(1)}, bf16[512,1024]{1,0:T(8,128)(2,1)}, u32[]{:S(2)}, u32[]{:S(2)}) collective-permute-start(bf16[512,1024]{1,0:T(8,128)(2,1)S(1)} %constant_dynamic-slice_fusion.4), channel_id=1, source_target_pairs={{0,1},{3,2},{4,5},{7,6},{8,9},{11,10},{12,13},{15,14},{16,17},{19,... | collective-permute-start | bytes 3145736 | tf_op jit(solution)/shard_map/ppermute | solution.py:286
  16.3 2.2 %copy.17 = bf16[16,8,64,128]{3,2,1,0:T(8,128)(2,1)S(1)} copy(bf16[16,8,64,128]{3,1,2,0:T(8,128)(2,1)} %bitcast.60) | data formatting | bytes 4194304
  18.5 7.0 %fusion.12 = (f32[128,8,8]{2,1,0:T(8,128)S(1)}, f32[128,8,8,32]{3,2,1,0:T(8,128)S(1)}) fusion(pred[128,32]{1,0:T(8,128)(4,1)S(1)} %iota_compare_fusion, bf16[128,8,8,128]{3,2,1,0:T(8,128)(2,1)S(1)} %bitcast.59, bf16[128,32,1024]{2,1,0:T(8,128)(2,1)} %param.13), kind=kOutput, calls=%fused_computation.17 | convolution fusion | flops 67887104 | bytes 11571200 | tf_op jit(solution)/shard_map/rkgd,rpkd->rkgp/dot_general | solution.py:28
  25.4 3.1 %fusion.13 = f32[128,8,8]{2,1,0:T(8,128)S(1)} fusion(f32[128,8,8,32]{3,2,1,0:T(8,128)S(1)} %get-tuple-element.69, f32[128,8,8]{2,1,0:T(8,128)S(1)} %get-tuple-element.68, pred[128,32]{1,0:T(8,128)(4,1)S(1)} %iota_compare_fusion), kind=kLoop, calls=%fused_computation.18 | loop fusion | flops 1302528 | bytes 1118208 | tf_op jit(solution)/shard_map/reduce_sum | solution.py:35
  28.5 6.0 %divide_convert_fusion = bf16[128,8,8,128]{3,2,1,0:T(8,128)(2,1)S(1)} fusion(f32[128,8,8]{2,1,0:T(8,128)S(1)} %fusion.13, f32[128,8,8,32]{3,2,1,0:T(8,128)S(1)} %get-tuple-element.69, f32[128,8,8]{2,1,0:T(8,128)S(1)} %get-tuple-element.68, pred[128,32]{1,0:T(8,128)(4,1)S(1)} %iota_compare_fusion, bf16[128,32,1024]{2,1,0:T(8,128)(2,1)} %param.14), kind=kOutput, calls=%fused_computation.14 | convolution fusion | flops 70254592 | bytes 11603968 | tf_op jit(solution)/shard_map/rkgp,rpkd->rkgd/dot_general | solution.py:36
  34.6 3.2 %copy.32 = bf16[16,8,64,128]{3,1,2,0:T(8,128)(2,1)} copy(bf16[16,8,64,128]{3,2,1,0:T(8,128)(2,1)S(1)} %bitcast.61) | data formatting | bytes 4194304
  38.9 1.6 copy-done.7
  41.6 2.0 %broadcast_select_fusion.2 = (bf16[64,4096]{1,0:T(8,128)(2,1)S(1)}, bf16[64,4096]{1,0:T(8,128)(2,1)S(1)}, bf16[64,4096]{1,0:T(8,128)(2,1)S(1)}, bf16[64,4096]{1,...) fusion(pred[]{:T(512)S(6)} %or.3, bf16[128,8192]{1,0:T(8,128)(2,1)} %bitcast.56, ...), kind=kLoop, calls=%fused_computation.56 | loop fusion | flops 524288 | bytes 5242893 | tf_op jit(solution)/shard_map/jit(_where)/select_n | solution.py:300
  45.1 1.8 collective-permute-start.3
  47.6 3.2 %collective-permute-start.6 = (bf16[64,4096]{1,0:T(8,128)(2,1)S(1)}, bf16[64,4096]{1,0:T(8,128)(2,1)}, u32[]{:S(2)}, u32[]{:S(2)}) collective-permute-start(bf16[64,4096]{1,0:T(8,128)(2,1)S(1)} %get-tuple-element.36), channel_id=1, source_target_pairs={{0,1},{1,0},{2,3},{3,2},{4,5},{5,4},{6,7},{7,6},{8,9},{9,8},{10,11... | collective-permute-start | bytes 1572872 | tf_op jit(solution)/shard_map/ppermute | solution.py:301
  50.8 9.1 %collective-permute-done.3 = bf16[64,4096]{1,0:T(8,128)(2,1)S(1)} collective-permute-done((bf16[64,4096]{1,0:T(8,128)(2,1)S(1)}, bf16[64,4096]{1,0:T(8,128)(2,1)S(1)}, u32[]{:S(2)}, u32[]{:S(2)}) %collective-permute-start.3) | collective-permute-done | bytes 524320 | tf_op jit(solution)/shard_map/ppermute | solution.py:301
  59.9 1.5 collective-permute-start.9
  61.4 2.7 %collective-permute-start.14 = (bf16[64,4096]{1,0:T(8,128)(2,1)S(1)}, bf16[64,4096]{1,0:T(8,128)(2,1)}, u32[]{:S(2)}, u32[]{:S(2)}) collective-permute-start(bf16[64,4096]{1,0:T(8,128)(2,1)S(1)} %broadcast_select_fusion), channel_id=1, source_target_pairs={{0,1},{1,0},{2,3},{3,2},{4,5},{5,4},{6,7},{7,6},{8,9},{9,8},{10,11... | collective-permute-start | bytes 1572872 | tf_op jit(solution)/shard_map/ppermute | solution.py:308
  64.1 1.7 shard_map.119
  66.9 4.4 %collective-permute-done.6 = bf16[64,4096]{1,0:T(8,128)(2,1)} collective-permute-done((bf16[64,4096]{1,0:T(8,128)(2,1)S(1)}, bf16[64,4096]{1,0:T(8,128)(2,1)}, u32[]{:S(2)}, u32[]{:S(2)}) %collective-permute-start.6) | collective-permute-done | bytes 524320 | tf_op jit(solution)/shard_map/ppermute | solution.py:301
  71.3 1.5 collective-permute-start.7
  72.7 2.7 %collective-permute-start.13 = (bf16[64,4096]{1,0:T(8,128)(2,1)}, bf16[64,4096]{1,0:T(8,128)(2,1)}, u32[]{:S(2)}, u32[]{:S(2)}) collective-permute-start(bf16[64,4096]{1,0:T(8,128)(2,1)} %broadcast_select_fusion.1), channel_id=1, source_target_pairs={{0,1},{1,0},{2,3},{3,2},{4,5},{5,4},{6,7},{7,6},{8,9},{9,8},{10,11... | collective-permute-start | bytes 1572872 | tf_op jit(solution)/shard_map/ppermute | solution.py:308
  76.6 7.3 %fusion.10.early_ref = f32[256,1024]{1,0:T(8,128)} fusion(bf16[8192,1024]{1,0:T(8,128)(2,1)} %param.16, s32[]{:T(128)S(6)} %select_n.104, bf16[128,4096]{1,0:T(8,128)(2,1)S(1)} %get-tuple-element.32, bf16[64,4096]{1,0:T(8,128)(2,1)S(1)} %collective-permute-done.3, bf16[64,4096]{1,0:T(8,128)(2,1)} %collective-permute-done.6), kind=kOutput, calls=%fused_computation.12 | convolution fusion | flops 2153775104 | bytes 11534340 | tf_op jit(solution)/shard_map/dot_general | solution.py:251
  83.9 1.5 collective-permute-start.20
  86.7 5.2 %all-to-all-start = ((bf16[2,4,64,3072]{3,2,1,0:T(8,128)(2,1)}), bf16[2,4,64,3072]{3,2,1,0:T(8,128)(2,1)}, u32[]{:S(2)}, u32[]{:S(2)}) async-start(bf16[2,4,64,3072]{3,2,1,0:T(8,128)(2,1)} %copy-done.4), calls=%async_computation | async-start | bytes 6291456 | tf_op jit(solution)/shard_map/all_to_all | solution.py:195
  91.9 1.6 collective-permute-start.10
  93.5 1.5 collective-permute-start.11
  95.0 1.5 collective-permute-start.15
  96.5 2.0 %select_dynamic-update-slice_fusion.5 = bf16[512,4096]{1,0:T(8,128)(2,1)} fusion(bf16[512,4096]{1,0:T(8,128)(2,1)} %get-tuple-element.61, bf16[64,4096]{1,0:T(8,128)(2,1)} %collective-permute-done.6, bf16[64,4096]{1,0:T(8,128)(2,1)} %collective-permute-done.13, pred[]{:T(512)S(6)} %or.3), kind=kLoop, calls=%fused_computation.53 | loop fusion | flops 262144 | bytes 1572865
  98.5 2.0 %select_dynamic-update-slice_fusion.4 = bf16[512,4096]{1,0:T(8,128)(2,1)} fusion(bf16[512,4096]{1,0:T(8,128)(2,1)} %select_dynamic-update-slice_fusion.5, bf16[64,4096]{1,0:T(8,128)(2,1)} %copy-done.20, bf16[64,4096]{1,0:T(8,128)(2,1)} %collective-permute-done.14, pred[]{:T(512)S(6)} %or.3), kind=kLoop, calls=%fused_computation.52 | loop fusion | flops 262144 | bytes 1572865
  100.5 2.0 %select_dynamic-update-slice_fusion.3 = bf16[512,4096]{1,0:T(8,128)(2,1)} fusion(bf16[512,4096]{1,0:T(8,128)(2,1)} %select_dynamic-update-slice_fusion.4, bf16[64,4096]{1,0:T(8,128)(2,1)} %collective-permute-done.13, bf16[64,4096]{1,0:T(8,128)(2,1)} %copy-done.17, pred[]{:T(512)S(6)} %or.3), kind=kLoop, calls=%fused_computation.51 | loop fusion | flops 262144 | bytes 1572865
  102.4 1.9 %select_dynamic-update-slice_fusion.2 = bf16[512,4096]{1,0:T(8,128)(2,1)} fusion(bf16[512,4096]{1,0:T(8,128)(2,1)} %select_dynamic-update-slice_fusion.3, bf16[64,4096]{1,0:T(8,128)(2,1)} %collective-permute-done.14, bf16[64,4096]{1,0:T(8,128)(2,1)S(1)} %copy-done.16, pred[]{:T(512)S(6)} %or.3), kind=kLoop, calls=%fused_computation.50 | loop fusion | flops 262144 | bytes 1572865
  104.4 10.8 %collective-permute-done.15 = bf16[64,4096]{1,0:T(8,128)(2,1)S(1)} collective-permute-done((bf16[64,4096]{1,0:T(8,128)(2,1)}, bf16[64,4096]{1,0:T(8,128)(2,1)S(1)}, u32[]{:S(2)}, u32[]{:S(2)}) %collective-permute-start.15) | collective-permute-done | bytes 524320 | tf_op jit(solution)/shard_map/ppermute | solution.py:317
  115.2 1.5 collective-permute-start.19
  117.6 2.0 %select_dynamic-update-slice_fusion = bf16[512,4096]{1,0:T(8,128)(2,1)} fusion(bf16[512,4096]{1,0:T(8,128)(2,1)} %select_dynamic-update-slice_fusion.1, bf16[64,4096]{1,0:T(8,128)(2,1)} %collective-permute-done.16, bf16[64,4096]{1,0:T(8,128)(2,1)} %collective-permute-done.9, pred[]{:T(512)S(6)} %or.3), kind=kLoop, calls=%fused_computation.48 | loop fusion | flops 262144 | bytes 1572865 | tf_op jit(solution)/shard_map/concatenate | solution.py:321
  119.6 3.2 %constant_dynamic-slice_fusion.3 = bf16[512,2048]{1,0:T(8,128)(2,1)} fusion(bf16[512,4096]{1,0:T(8,128)(2,1)} %select_dynamic-update-slice_fusion, s32[]{:T(128)S(6)} %select_n.119), kind=kLoop, calls=%fused_computation.67 | loop fusion | bytes 4194308 | tf_op jit(solution)/shard_map/dynamic_slice | solution.py:333
  122.8 4.0 %all-to-all-done.fetched_ref = bf16[2,4,64,3072]{3,2,1,0:T(8,128)(2,1)} async-done(((bf16[2,4,64,3072]{3,2,1,0:T(8,128)(2,1)}), bf16[2,4,64,3072]{3,2,1,0:T(8,128)(2,1)}, u32[]{:S(2)}, u32[]{:S(2)}) %all-to-all-start) | async-done | bytes 3145760 | tf_op jit(solution)/shard_map/all_to_all | solution.py:195
  126.8 1.4 copy-done.3
  128.2 2.0 %shard_map.120.refs_4_ = bf16[4,64,3072]{2,1,0:T(8,128)(2,1)S(1)} custom-call(s32[1]{0:T(128)} %bitcast.2.here_ref, s32[4,4]{1,0:T(4,128)S(1)} %pad_add_fusion.ids_ref, s32[48]{0:T(128)S(1)} %copy-done.9, s32[4]{0:T(128)S(1)} %fusion.49.order_ref, bf16[12,64,2048]{2,1,0:T(8,128)(2,1)S(1)} %bitcast.55, bf16[12,64,1024]{2,1,0:T(8,128)(2,1)S(1)} %copy-done.3, ...), custom_call_target="tpu_custom_call" | custom-call | tf_op jit(solution)/shard_map/pallas_call | solution.py:203
  132.7 3.1 %collective-permute-start.17 = (f32[4,64,128]{2,1,0:T(8,128)S(1)}, f32[4,64,128]{2,1,0:T(8,128)S(1)}, u32[]{:S(2)}, u32[]{:S(2)}) collective-permute-start(f32[4,64,128]{2,1,0:T(8,128)S(1)} %gather_fusion), channel_id=1, source_target_pairs={{0,1},{1,0},{2,3},{3,2},{4,5},{5,4},{6,7},{7,6},{8,9},{9,8},{10,11... | collective-permute-start | bytes 393224 | tf_op jit(solution)/shard_map/ppermute | solution.py:218
  135.8 8.1 %fusion.6.near_ref = f32[512,1024]{1,0:T(8,128)S(1)} fusion(bf16[512,4096]{1,0:T(8,128)(2,1)} %select_dynamic-update-slice_fusion, bf16[8192,1024]{1,0:T(8,128)(2,1)} %param.16, s32[]{:T(128)S(6)} %select_n.106), kind=kOutput, calls=%fused_computation.8 | convolution fusion | flops 4294967296 | bytes 14680068 | tf_op jit(solution)/shard_map/dot_general | solution.py:251
  144.9 2.3 %pad_maximum_fusion.2 = bf16[128,4096]{1,0:T(8,128)(2,1)} fusion(bf16[64,4096]{1,0:T(8,128)(2,1)} %collective-permute-done.11, bf16[64,4096]{1,0:T(8,128)(2,1)} %collective-permute-done.10), kind=kLoop, calls=%fused_computation.43 | loop fusion | flops 2097152 | bytes 2097152 | tf_op jit(solution)/shard_map/concatenate | solution.py:345
  147.2 3.6 %collective-permute-done.18 = f32[4,64,128]{2,1,0:T(8,128)S(1)} collective-permute-done((f32[4,64,128]{2,1,0:T(8,128)S(1)}, f32[4,64,128]{2,1,0:T(8,128)S(1)}, u32[]{:S(2)}, u32[]{:S(2)}) %collective-permute-start.18) | collective-permute-done | bytes 131104 | tf_op jit(solution)/shard_map/ppermute | solution.py:218
  151.5 6.5 %fusion.33 = bf16[256,1024]{1,0:T(8,128)(2,1)S(1)} fusion(bf16[4096,1024]{1,0:T(8,128)(2,1)} %all-gather.2.cloned.1.call-done, bf16[128,4096]{1,0:T(8,128)(2,1)} %copy-done.18, bf16[64,4096]{1,0:T(8,128)(2,1)} %collective-permute-done.11, bf16[64,4096]{1,0:T(8,128)(2,1)} %collective-permute-done.10), kind=kOutput, calls=%fused_computation.39 | convolution fusion | flops 2154037248 | bytes 11010048 | tf_op jit(solution)/shard_map/dot_general | solution.py:251
  158.0 1.6 collective-permute-start.21
  159.6 3.4 %convolution_convert_fusion = bf16[128,1024]{1,0:T(8,128)(2,1)S(1)} fusion(bf16[4096,1024]{1,0:T(8,128)(2,1)S(1)} %copy-done.22, bf16[64,4096]{1,0:T(8,128)(2,1)} %collective-permute-done.20, bf16[64,4096]{1,0:T(8,128)(2,1)} %collective-permute-done.19), kind=kOutput, calls=%fused_computation.40 | convolution fusion | flops 1075970048 | bytes 9699328 | tf_op jit(solution)/shard_map/dot_general | solution.py:251
  163.0 1.4 collective-permute-start.22
  164.5 3.6 %fusion.8.late_ref = f32[256,1024]{1,0:T(8,128)S(1)} fusion(bf16[8192,1024]{1,0:T(8,128)(2,1)S(1)} %bitcast.63, s32[]{:T(128)S(6)} %select_n.104, bf16[64,4096]{1,0:T(8,128)(2,1)} %collective-permute-done.20, bf16[64,4096]{1,0:T(8,128)(2,1)} %collective-permute-done.19, bf16[128,4096]{1,0:T(8,128)(2,1)S(1)} %copy-done.19), kind=kOutput, calls=%fused_computation.10 | convolution fusion | flops 2153775104 | bytes 11534340 | tf_op jit(solution)/shard_map/dot_general | solution.py:251
  168.1 4.6 %collective-permute-done.21 = bf16[256,1024]{1,0:T(8,128)(2,1)S(1)} collective-permute-done((bf16[256,1024]{1,0:T(8,128)(2,1)S(1)}, bf16[256,1024]{1,0:T(8,128)(2,1)S(1)}, u32[]{:S(2)}, u32[]{:S(2)}) %collective-permute-start.21) | collective-permute-done | bytes 524320 | tf_op jit(solution)/shard_map/ppermute | solution.py:347
  172.7 2.8 %collective-permute-done.22.refs_2_ = bf16[128,1024]{1,0:T(8,128)(2,1)S(1)} collective-permute-done((bf16[128,1024]{1,0:T(8,128)(2,1)S(1)}, bf16[128,1024]{1,0:T(8,128)(2,1)S(1)}, u32[]{:S(2)}, u32[]{:S(2)}) %collective-permute-start.22) | collective-permute-done | bytes 262176 | tf_op jit(solution)/shard_map/ppermute | solution.py:351
  175.5 2.2 %shard_map.121 = bf16[512,1024]{1,0:T(8,128)(2,1)} custom-call(s32[4]{0:T(128)S(1)} %fusion.49.order_ref, s32[4]{0:T(128)S(1)} %copy-done.10, s32[1]{0:T(128)} %bitcast.1.end_ref, f32[512,1024]{1,0:T(8,128)S(1)} %fusion.6.near_ref, f32[256,1024]{1,0:T(8,128)S(1)} %copy-done.8, f32[256,1024]{1,0:T(8,128)S(1)} %fusion.8.late_ref, ...), custom_call_target="tpu_custom_call" | custom-call | tf_op jit(solution)/shard_map/pallas_call | solution.py:354
  (100 shorter events, 14.5 us)
Async XLA Ops:
  6.5 144.9 %all-gather.2.cloned.1.call-start = ((), (), s32[]{:S(2)}) async-start(), calls=%async_computation.1 | async-start | bytes 9437184 | tf_op jit(solution)/shard_map/all_gather | solution.py:293
  6.5 31.2 %collective-permute-start = (s32[4]{0:T(128)}, s32[4]{0:T(128)S(1)}, u32[]{:S(2)}, u32[]{:S(2)}) collective-permute-start(s32[4]{0:T(128)} %param.19), channel_id=1, source_target_pairs={{0,12},{4,0},{8,4},{12,8},{1,13},{5,1},{9,5},{13,9},{2,14},{6,2},{... | collective-permute-start | bytes 56 | tf_op jit(solution)/shard_map/ppermute | solution.py:160
  8.9 28.8 %collective-permute-start.1 = (s32[4]{0:T(128)}, s32[4]{0:T(128)S(1)}, u32[]{:S(2)}, u32[]{:S(2)}) collective-permute-start(s32[4]{0:T(128)} %param.19), channel_id=1, source_target_pairs={{0,8},{4,12},{8,0},{12,4},{1,9},{5,13},{9,1},{13,5},{2,10},{6,14},... | collective-permute-start | bytes 56 | tf_op jit(solution)/shard_map/ppermute | solution.py:160
  9.5 28.3 %collective-permute-start.2 = (s32[4]{0:T(128)}, s32[4]{0:T(128)S(1)}, u32[]{:S(2)}, u32[]{:S(2)}) collective-permute-start(s32[4]{0:T(128)} %param.19), channel_id=1, source_target_pairs={{0,4},{4,8},{8,12},{12,0},{1,5},{5,9},{9,13},{13,1},{2,6},{6,10},{... | collective-permute-start | bytes 56 | tf_op jit(solution)/shard_map/ppermute | solution.py:160
  11.0 29.5 %collective-permute-start.12 = (bf16[512,1024]{1,0:T(8,128)(2,1)S(1)}, bf16[512,1024]{1,0:T(8,128)(2,1)}, u32[]{:S(2)}, u32[]{:S(2)}) collective-permute-start(bf16[512,1024]{1,0:T(8,128)(2,1)S(1)} %constant_dynamic-slice_fusion.4), channel_id=1, source_target_pairs={{0,1},{3,2},{4,5},{7,6},{8,9},{11,10},{12,13},{15,14},{16,17},{19,... | collective-permute-start | bytes 3145736 | tf_op jit(solution)/shard_map/ppermute | solution.py:286
  28.5 9.3 %copy-start.1 = (bf16[12,64,1024]{2,1,0:T(8,128)(2,1)S(1)}, bf16[12,64,1024]{2,1,0:T(8,128)(2,1)}, u32[]{:S(2)}) copy-start(bf16[12,64,1024]{2,1,0:T(8,128)(2,1)} %up_ref.5) | copy-start | bytes 4718596
  34.5 3.3 %copy-start = (bf16[12,2048,64]{1,2,0:T(8,128)(2,1)S(1)}, bf16[12,2048,64]{1,2,0:T(8,128)(2,1)}, u32[]{:S(2)}) copy-start(bf16[12,2048,64]{1,2,0:T(8,128)(2,1)} %param.17) | copy-start | bytes 9437188
  34.5 3.3 %copy-start.9 = (s32[48]{0:T(128)S(1)}, s32[48]{0:T(128)}, u32[]{:S(2)}) copy-start(s32[48]{0:T(128)} %slots_ref.5) | copy-start | bytes 580
  40.5 3.8 %copy-start.23 = (s32[4,4]{1,0:T(4,128)S(1)}, s32[4,4]{1,0:T(4,128)}, u32[]{:S(2)}) copy-start(s32[4,4]{1,0:T(4,128)} %constant.65.clone) | copy-start | bytes 196
  40.6 23.5 %collective-permute-start.5 = (bf16[2,4,64,3072]{3,2,1,0:T(8,128)(2,1)}, bf16[2,4,64,3072]{3,2,1,0:T(8,128)(2,1)}, u32[]{:S(2)}, u32[]{:S(2)}) collective-permute-start(bf16[2,4,64,3072]{3,2,1,0:T(8,128)(2,1)} %copy-done.7), channel_id=1, source_target_pairs={{0,4},{4,0},{8,12},{12,8},{1,5},{5,1},{9,13},{13,9},{2,6},{6,2},{1... | collective-permute-start | bytes 9437192 | tf_op jit(solution)/shard_map/ppermute | solution.py:180
  41.6 22.5 %copy-start.2 = (bf16[12,64,1024]{2,1,0:T(8,128)(2,1)S(1)}, bf16[12,64,1024]{2,1,0:T(8,128)(2,1)}, u32[]{:S(2)}) copy-start(bf16[12,64,1024]{2,1,0:T(8,128)(2,1)} %up_ref.5) | copy-start | bytes 4718596
  43.6 20.5 %copy-start.13 = (bf16[64,4096]{1,0:T(8,128)(2,1)}, bf16[64,4096]{1,0:T(8,128)(2,1)S(1)}, u32[]{:S(2)}) copy-start(bf16[64,4096]{1,0:T(8,128)(2,1)S(1)} %get-tuple-element.41) | copy-start | bytes 1572868
  43.6 22.3 %copy-start.14 = (bf16[64,4096]{1,0:T(8,128)(2,1)}, bf16[64,4096]{1,0:T(8,128)(2,1)S(1)}, u32[]{:S(2)}) copy-start(bf16[64,4096]{1,0:T(8,128)(2,1)S(1)} %get-tuple-element.40) | copy-start | bytes 1572868
  43.6 7.1 %collective-permute-start.8 = (bf16[64,4096]{1,0:T(8,128)(2,1)S(1)}, bf16[64,4096]{1,0:T(8,128)(2,1)S(1)}, u32[]{:S(2)}, u32[]{:S(2)}) collective-permute-start(bf16[64,4096]{1,0:T(8,128)(2,1)S(1)} %get-tuple-element.38), channel_id=1, source_target_pairs={{1,2},{2,1},{5,6},{6,5},{9,10},{10,9},{13,14},{14,13},{17,18},{18,... | collective-permute-start | bytes 1572872 | tf_op jit(solution)/shard_map/ppermute | solution.py:302
  45.1 14.8 %collective-permute-start.3 = (bf16[64,4096]{1,0:T(8,128)(2,1)S(1)}, bf16[64,4096]{1,0:T(8,128)(2,1)S(1)}, u32[]{:S(2)}, u32[]{:S(2)}) collective-permute-start(bf16[64,4096]{1,0:T(8,128)(2,1)S(1)} %get-tuple-element.31), channel_id=1, source_target_pairs={{0,1},{1,0},{2,3},{3,2},{4,5},{5,4},{6,7},{7,6},{8,9},{9,8},{10,11... | collective-permute-start | bytes 1572872 | tf_op jit(solution)/shard_map/ppermute | solution.py:301
  46.9 19.0 %collective-permute-start.4 = (bf16[64,4096]{1,0:T(8,128)(2,1)S(1)}, bf16[64,4096]{1,0:T(8,128)(2,1)S(1)}, u32[]{:S(2)}, u32[]{:S(2)}) collective-permute-start(bf16[64,4096]{1,0:T(8,128)(2,1)S(1)} %get-tuple-element.33), channel_id=1, source_target_pairs={{1,2},{2,1},{5,6},{6,5},{9,10},{10,9},{13,14},{14,13},{17,18},{18,... | collective-permute-start | bytes 1572872 | tf_op jit(solution)/shard_map/ppermute | solution.py:302
  47.6 23.7 %collective-permute-start.6 = (bf16[64,4096]{1,0:T(8,128)(2,1)S(1)}, bf16[64,4096]{1,0:T(8,128)(2,1)}, u32[]{:S(2)}, u32[]{:S(2)}) collective-permute-start(bf16[64,4096]{1,0:T(8,128)(2,1)S(1)} %get-tuple-element.36), channel_id=1, source_target_pairs={{0,1},{1,0},{2,3},{3,2},{4,5},{5,4},{6,7},{7,6},{8,9},{9,8},{10,11... | collective-permute-start | bytes 1572872 | tf_op jit(solution)/shard_map/ppermute | solution.py:301
  50.7 13.4 %copy-start.15 = (bf16[64,4096]{1,0:T(8,128)(2,1)}, bf16[64,4096]{1,0:T(8,128)(2,1)S(1)}, u32[]{:S(2)}) copy-start(bf16[64,4096]{1,0:T(8,128)(2,1)S(1)} %collective-permute-done.8) | copy-start | bytes 1572868
  50.8 24.6 %copy-start.11 = (bf16[16,8,64,128]{3,1,2,0:T(8,128)(2,1)S(1)}, bf16[16,8,64,128]{3,1,2,0:T(8,128)(2,1)}, u32[]{:S(2)}) copy-start(bf16[16,8,64,128]{3,1,2,0:T(8,128)(2,1)} %copy.32) | copy-start | bytes 6291460
  59.9 16.7 %copy-start.20 = (bf16[64,4096]{1,0:T(8,128)(2,1)}, bf16[64,4096]{1,0:T(8,128)(2,1)S(1)}, u32[]{:S(2)}) copy-start(bf16[64,4096]{1,0:T(8,128)(2,1)S(1)} %collective-permute-done.3) | copy-start | bytes 1572868
  59.9 25.4 %collective-permute-start.9 = (bf16[64,4096]{1,0:T(8,128)(2,1)S(1)}, bf16[64,4096]{1,0:T(8,128)(2,1)}, u32[]{:S(2)}, u32[]{:S(2)}) collective-permute-start(bf16[64,4096]{1,0:T(8,128)(2,1)S(1)} %collective-permute-done.3), channel_id=1, source_target_pairs={{1,2},{2,1},{5,6},{6,5},{9,10},{10,9},{13,14},{14,13},{17,18},{18,... | collective-permute-start | bytes 1572872 | tf_op jit(solution)/shard_map/ppermute | solution.py:309
  61.4 22.5 %collective-permute-start.14 = (bf16[64,4096]{1,0:T(8,128)(2,1)S(1)}, bf16[64,4096]{1,0:T(8,128)(2,1)}, u32[]{:S(2)}, u32[]{:S(2)}) collective-permute-start(bf16[64,4096]{1,0:T(8,128)(2,1)S(1)} %broadcast_select_fusion), channel_id=1, source_target_pairs={{0,1},{1,0},{2,3},{3,2},{4,5},{5,4},{6,7},{7,6},{8,9},{9,8},{10,11... | collective-permute-start | bytes 1572872 | tf_op jit(solution)/shard_map/ppermute | solution.py:308
  65.9 18.0 %copy-start.4 = (bf16[2,4,64,3072]{3,2,1,0:T(8,128)(2,1)}, bf16[2,4,64,3072]{3,2,1,0:T(8,128)(2,1)S(1)}, u32[]{:S(2)}) copy-start(bf16[2,4,64,3072]{3,2,1,0:T(8,128)(2,1)S(1)} %shard_map.119) | copy-start | bytes 9437188
  65.9 18.0 %copy-start.17 = (bf16[64,4096]{1,0:T(8,128)(2,1)}, bf16[64,4096]{1,0:T(8,128)(2,1)S(1)}, u32[]{:S(2)}) copy-start(bf16[64,4096]{1,0:T(8,128)(2,1)S(1)} %collective-permute-done.4) | copy-start | bytes 1572868
  71.3 20.6 %collective-permute-start.7 = (bf16[64,4096]{1,0:T(8,128)(2,1)}, bf16[64,4096]{1,0:T(8,128)(2,1)}, u32[]{:S(2)}, u32[]{:S(2)}) collective-permute-start(bf16[64,4096]{1,0:T(8,128)(2,1)} %collective-permute-done.6), channel_id=1, source_target_pairs={{1,2},{2,1},{5,6},{6,5},{9,10},{10,9},{13,14},{14,13},{17,18},{18,... | collective-permute-start | bytes 1572872 | tf_op jit(solution)/shard_map/ppermute | solution.py:309
  72.7 22.3 %collective-permute-start.13 = (bf16[64,4096]{1,0:T(8,128)(2,1)}, bf16[64,4096]{1,0:T(8,128)(2,1)}, u32[]{:S(2)}, u32[]{:S(2)}) collective-permute-start(bf16[64,4096]{1,0:T(8,128)(2,1)} %broadcast_select_fusion.1), channel_id=1, source_target_pairs={{0,1},{1,0},{2,3},{3,2},{4,5},{5,4},{6,7},{7,6},{8,9},{9,8},{10,11... | collective-permute-start | bytes 1572872 | tf_op jit(solution)/shard_map/ppermute | solution.py:308
  76.6 7.3 %copy-start.18 = (bf16[128,4096]{1,0:T(8,128)(2,1)}, bf16[128,4096]{1,0:T(8,128)(2,1)S(1)}, u32[]{:S(2)}) copy-start(bf16[128,4096]{1,0:T(8,128)(2,1)S(1)} %get-tuple-element.32) | copy-start | bytes 3145732
  83.9 75.7 %collective-permute-start.20 = (bf16[64,4096]{1,0:T(8,128)(2,1)}, bf16[64,4096]{1,0:T(8,128)(2,1)}, u32[]{:S(2)}, u32[]{:S(2)}) collective-permute-start(bf16[64,4096]{1,0:T(8,128)(2,1)} %collective-permute-done.14), channel_id=1, source_target_pairs={{1,2},{2,1},{5,6},{6,5},{9,10},{10,9},{13,14},{14,13},{17,18},{18,... | collective-permute-start | bytes 1572872 | tf_op jit(solution)/shard_map/ppermute | solution.py:319
  85.4 32.2 %collective-permute-start.16 = (bf16[64,4096]{1,0:T(8,128)(2,1)}, bf16[64,4096]{1,0:T(8,128)(2,1)}, u32[]{:S(2)}, u32[]{:S(2)}) collective-permute-start(bf16[64,4096]{1,0:T(8,128)(2,1)} %collective-permute-done.9), channel_id=1, source_target_pairs={{1,0},{2,3},{5,4},{6,7},{9,8},{10,11},{13,12},{14,15},{17,16},{18,... | collective-permute-start | bytes 1572872 | tf_op jit(solution)/shard_map/ppermute | solution.py:317
  86.7 40.1 %all-to-all-start = ((bf16[2,4,64,3072]{3,2,1,0:T(8,128)(2,1)}), bf16[2,4,64,3072]{3,2,1,0:T(8,128)(2,1)}, u32[]{:S(2)}, u32[]{:S(2)}) async-start(bf16[2,4,64,3072]{3,2,1,0:T(8,128)(2,1)} %copy-done.4), calls=%async_computation | async-start | bytes 6291456 | tf_op jit(solution)/shard_map/all_to_all | solution.py:195
  91.9 10.6 %copy-start.16 = (bf16[64,4096]{1,0:T(8,128)(2,1)S(1)}, bf16[64,4096]{1,0:T(8,128)(2,1)}, u32[]{:S(2)}) copy-start(bf16[64,4096]{1,0:T(8,128)(2,1)} %copy-done.15) | copy-start | bytes 1572868
  91.9 53.1 %collective-permute-start.10 = (bf16[64,4096]{1,0:T(8,128)(2,1)}, bf16[64,4096]{1,0:T(8,128)(2,1)}, u32[]{:S(2)}, u32[]{:S(2)}) collective-permute-start(bf16[64,4096]{1,0:T(8,128)(2,1)} %copy-done.14), channel_id=1, source_target_pairs={{1,2},{2,1},{5,6},{6,5},{9,10},{10,9},{13,14},{14,13},{17,18},{18,... | collective-permute-start | bytes 1572872 | tf_op jit(solution)/shard_map/ppermute | solution.py:318
  93.5 51.5 %collective-permute-start.11 = (bf16[64,4096]{1,0:T(8,128)(2,1)}, bf16[64,4096]{1,0:T(8,128)(2,1)}, u32[]{:S(2)}, u32[]{:S(2)}) collective-permute-start(bf16[64,4096]{1,0:T(8,128)(2,1)} %copy-done.13), channel_id=1, source_target_pairs={{1,2},{2,1},{5,6},{6,5},{9,10},{10,9},{13,14},{14,13},{17,18},{18,... | collective-permute-start | bytes 1572872 | tf_op jit(solution)/shard_map/ppermute | solution.py:318
  95.0 20.2 %collective-permute-start.15 = (bf16[64,4096]{1,0:T(8,128)(2,1)}, bf16[64,4096]{1,0:T(8,128)(2,1)S(1)}, u32[]{:S(2)}, u32[]{:S(2)}) collective-permute-start(bf16[64,4096]{1,0:T(8,128)(2,1)} %collective-permute-done.7), channel_id=1, source_target_pairs={{1,0},{2,3},{5,4},{6,7},{9,8},{10,11},{13,12},{14,15},{17,16},{18,... | collective-permute-start | bytes 1572872 | tf_op jit(solution)/shard_map/ppermute | solution.py:317
  115.2 44.4 %collective-permute-start.19 = (bf16[64,4096]{1,0:T(8,128)(2,1)}, bf16[64,4096]{1,0:T(8,128)(2,1)}, u32[]{:S(2)}, u32[]{:S(2)}) collective-permute-start(bf16[64,4096]{1,0:T(8,128)(2,1)} %collective-permute-done.13), channel_id=1, source_target_pairs={{1,2},{2,1},{5,6},{6,5},{9,10},{10,9},{13,14},{14,13},{17,18},{18,... | collective-permute-start | bytes 1572872 | tf_op jit(solution)/shard_map/ppermute | solution.py:319
  132.7 11.3 %collective-permute-start.17 = (f32[4,64,128]{2,1,0:T(8,128)S(1)}, f32[4,64,128]{2,1,0:T(8,128)S(1)}, u32[]{:S(2)}, u32[]{:S(2)}) collective-permute-start(f32[4,64,128]{2,1,0:T(8,128)S(1)} %gather_fusion), channel_id=1, source_target_pairs={{0,1},{1,0},{2,3},{3,2},{4,5},{5,4},{6,7},{7,6},{8,9},{9,8},{10,11... | collective-permute-start | bytes 393224 | tf_op jit(solution)/shard_map/ppermute | solution.py:218
  144.0 6.8 %collective-permute-start.18 = (f32[4,64,128]{2,1,0:T(8,128)S(1)}, f32[4,64,128]{2,1,0:T(8,128)S(1)}, u32[]{:S(2)}, u32[]{:S(2)}) collective-permute-start(f32[4,64,128]{2,1,0:T(8,128)S(1)} %add.64), channel_id=1, source_target_pairs={{0,2},{1,3},{2,0},{3,1},{4,6},{5,7},{6,4},{7,5},{8,10},{9,11},{10,... | collective-permute-start | bytes 393224 | tf_op jit(solution)/shard_map/ppermute | solution.py:218
  151.4 8.2 %copy-start.22 = (bf16[4096,1024]{1,0:T(8,128)(2,1)S(1)}, bf16[4096,1024]{1,0:T(8,128)(2,1)}, u32[]{:S(2)}) copy-start(bf16[4096,1024]{1,0:T(8,128)(2,1)} %all-gather.2.cloned.1.call-done) | copy-start | bytes 25165828
  151.4 13.0 %slice-start = ((s8[16777216]{0:T(1024)(128)(4,1)}), s8[4194304]{0:T(1024)(128)(4,1)S(1)}, s32[]{:S(2)}) async-start(s8[16777216]{0:T(1024)(128)(4,1)} %bitcast.62), calls=%async_computation.2 | async-start | bytes 8388608
  151.5 13.0 %slice-start.1 = ((s8[16777216]{0:T(1024)(128)(4,1)}), s8[4194304]{0:T(1024)(128)(4,1)S(1)}, s32[]{:S(2)}) async-start(s8[16777216]{0:T(1024)(128)(4,1)} %bitcast.62), calls=%async_computation.3 | async-start | bytes 8388608
  151.5 13.0 %slice-start.2 = ((s8[16777216]{0:T(1024)(128)(4,1)}), s8[4194304]{0:T(1024)(128)(4,1)S(1)}, s32[]{:S(2)}) async-start(s8[16777216]{0:T(1024)(128)(4,1)} %bitcast.62), calls=%async_computation.4 | async-start | bytes 8388608
  158.0 6.5 %copy-start.19 = (bf16[128,4096]{1,0:T(8,128)(2,1)S(1)}, bf16[128,4096]{1,0:T(8,128)(2,1)}, u32[]{:S(2)}) copy-start(bf16[128,4096]{1,0:T(8,128)(2,1)} %pad_maximum_fusion.2) | copy-start | bytes 3145732
  158.0 6.5 %slice-start.3 = ((s8[16777216]{0:T(1024)(128)(4,1)}), s8[4194304]{0:T(1024)(128)(4,1)S(1)}, s32[]{:S(2)}) async-start(s8[16777216]{0:T(1024)(128)(4,1)} %bitcast.62), calls=%async_computation.5 | async-start | bytes 8388608
  158.0 14.7 %collective-permute-start.21 = (bf16[256,1024]{1,0:T(8,128)(2,1)S(1)}, bf16[256,1024]{1,0:T(8,128)(2,1)S(1)}, u32[]{:S(2)}, u32[]{:S(2)}) collective-permute-start(bf16[256,1024]{1,0:T(8,128)(2,1)S(1)} %fusion.33), channel_id=1, source_target_pairs={{1,0},{2,3},{5,4},{6,7},{9,8},{10,11},{13,12},{14,15},{17,16},{18,... | collective-permute-start | bytes 1572872 | tf_op jit(solution)/shard_map/ppermute | solution.py:347
  163.0 12.5 %copy-start.6 = (bf16[4,64,3072]{2,1,0:T(8,128)(2,1)S(1)}, bf16[4,64,3072]{2,1,0:T(8,128)(2,1)}, u32[]{:S(2)}) copy-start(bf16[4,64,3072]{2,1,0:T(8,128)(2,1)} %copy-done.5) | copy-start | bytes 4718596
  163.0 12.5 %copy-start.8 = (f32[256,1024]{1,0:T(8,128)S(1)}, f32[256,1024]{1,0:T(8,128)}, u32[]{:S(2)}) copy-start(f32[256,1024]{1,0:T(8,128)} %fusion.10.early_ref) | copy-start | bytes 3145732
  163.0 12.5 %copy-start.10 = (s32[4]{0:T(128)S(1)}, s32[4]{0:T(128)}, u32[]{:S(2)}) copy-start(s32[4]{0:T(128)} %live_ref.1) | copy-start | bytes 52
  163.0 12.5 %collective-permute-start.22 = (bf16[128,1024]{1,0:T(8,128)(2,1)S(1)}, bf16[128,1024]{1,0:T(8,128)(2,1)S(1)}, u32[]{:S(2)}, u32[]{:S(2)}) collective-permute-start(bf16[128,1024]{1,0:T(8,128)(2,1)S(1)} %convolution_convert_fusion), channel_id=1, source_target_pairs={{1,0},{2,3},{5,4},{6,7},{9,8},{10,11},{13,12},{14,15},{17,16},{18,... | collective-permute-start | bytes 786440 | tf_op jit(solution)/shard_map/ppermute | solution.py:351
  (5 other events, 9.4 us)
Sparse Core Ops, SparseCore 0:
  40.7 54.2 all-gather.1

commit v3 on v2

--- a/solution.py
+++ b/solution.py
@@ -313,7 +313,7 @@
     e2[-1], early_out = tie(e2[-1], early_out)
     m3, m4, e3 = [], [], []
     for p in range(PARTS):
-        inner, *_ = tie(nears[p], *m2)
+        inner, *_ = tie(nears[p], *m2, *e2[:1])
         e3.append(lax.ppermute(m2[p], "tensor", outward))
         m3.append(lax.ppermute(inner, "tensor", middle))
         m4.append(lax.ppermute(e2[p], "tensor", middle))
@@ -345,7 +345,7 @@
     inner = jnp.concatenate(m3)
     inner_sent = dot(jnp.concatenate([far, inner]), end_weight).astype(jnp.bfloat16)
     inner_passed = lax.ppermute(inner_sent, "tensor", outward)
-    inner_sent, near_out, reduced, *m4 = tie(inner_sent, near_out, reduced, *m4)
+    inner_sent, *m4 = tie(inner_sent, *m4)
     last = jnp.concatenate(m4)
     last_sent = dot(last, end_weight).astype(jnp.bfloat16)
     last_passed = lax.ppermute(last_sent, "tensor", outward)

time: 186 us -> 186 us (level)
    unnamed x59 -> x58, local copies, waits for them, and re-layouts: 10.8 us -> 9.65 us
  transfers between devices with their start and end apart: 25 -> 25, of which waited for: 7 -> 8; matrix products, arithmetic and copies ran while one was open for 41% -> 41% of each run, Pallas kernels for 3% -> 2%
where the time goes in v3:
time: 186 us; the launch traced here: 185 us
  starting transfers between devices  44.2 us (24%)
  matrix products  42.6 us (23%)
  waiting for transfers between devices  40.5 us (22%)
  other arithmetic  20.7 us (11%)
  local copies, waits for them, and re-layouts  16.5 us (9%)
  between operations  14 us (8%)
  Pallas kernels  6 us (3%)
    dot_general x5, matrix products, dot(): return jnp.dot(a, b, preferred_element_type=jnp.float32)  28.8 us
    ppermute x2, waiting for transfers between devices, line_body(): e1.append(lax.ppermute(outer, 'tensor', ends))  14.5 us
    unnamed x58, local copies, waits for them, and re-layouts  9.65 us
    ppermute x2, waiting for transfers between devices, line_body(): e3.append(lax.ppermute(m2[p], 'tensor', outward))  9.15 us
    unnamed x6, other arithmetic  8.84 us
    dot_general x1, matrix products, attention(): jnp.einsum('rkgd,rpkd->rkgp', query_heads, key_heads, preferred_element_t...  6.96 us
    dot_general x1, matrix products, attention(): summed = jnp.einsum('rkgp,rpkd->rkgd', weights, value_heads)  5.99 us
    ppermute x2, starting transfers between devices, line_body(): e2.append(lax.ppermute(outer, 'tensor', ends))  5.38 us
  transfers between devices with their start and end apart: 25, of which 8 were waited for; matrix products, arithmetic and copies ran while one was open for 41% of the time, Pallas kernels for 2%

profile of v3, /device:TPU:0, one launch (start us, length us, event | category | flops | bytes accessed | tf_op | source)
XLA Modules:
  0.0 184.6 jit_solution(5692728686151287113)
XLA Ops:
  6.5 2.4 %collective-permute-start = (s32[4]{0:T(128)}, s32[4]{0:T(128)S(1)}, u32[]{:S(2)}, u32[]{:S(2)}) collective-permute-start(s32[4]{0:T(128)} %param.19), channel_id=1, source_target_pairs={{0,12},{4,0},{8,4},{12,8},{1,13},{5,1},{9,5},{13,9},{2,14},{6,2},{... | collective-permute-start | bytes 56 | tf_op jit(solution)/shard_map/ppermute | solution.py:160
  9.7 1.3 constant_dynamic-slice_fusion.3
  11.0 4.5 %collective-permute-start.16 = (bf16[512,1024]{1,0:T(8,128)(2,1)S(1)}, bf16[512,1024]{1,0:T(8,128)(2,1)}, u32[]{:S(2)}, u32[]{:S(2)}) collective-permute-start(bf16[512,1024]{1,0:T(8,128)(2,1)S(1)} %constant_dynamic-slice_fusion.3), channel_id=1, source_target_pairs={{0,1},{3,2},{4,5},{7,6},{8,9},{11,10},{12,13},{15,14},{16,17},{19,... | collective-permute-start | bytes 3145736 | tf_op jit(solution)/shard_map/ppermute | solution.py:286
  16.3 2.2 %copy.17 = bf16[16,8,64,128]{3,2,1,0:T(8,128)(2,1)S(1)} copy(bf16[16,8,64,128]{3,1,2,0:T(8,128)(2,1)} %bitcast.60) | data formatting | bytes 4194304
  18.5 7.0 %fusion.12 = (f32[128,8,8]{2,1,0:T(8,128)S(1)}, f32[128,8,8,32]{3,2,1,0:T(8,128)S(1)}) fusion(pred[128,32]{1,0:T(8,128)(4,1)S(1)} %iota_compare_fusion, bf16[128,8,8,128]{3,2,1,0:T(8,128)(2,1)S(1)} %bitcast.59, bf16[128,32,1024]{2,1,0:T(8,128)(2,1)} %param.13), kind=kOutput, calls=%fused_computation.17 | convolution fusion | flops 67887104 | bytes 11571200 | tf_op jit(solution)/shard_map/rkgd,rpkd->rkgp/dot_general | solution.py:28
  25.4 3.1 %fusion.13 = f32[128,8,8]{2,1,0:T(8,128)S(1)} fusion(f32[128,8,8,32]{3,2,1,0:T(8,128)S(1)} %get-tuple-element.65, f32[128,8,8]{2,1,0:T(8,128)S(1)} %get-tuple-element.64, pred[128,32]{1,0:T(8,128)(4,1)S(1)} %iota_compare_fusion), kind=kLoop, calls=%fused_computation.18 | loop fusion | flops 1302528 | bytes 1118208 | tf_op jit(solution)/shard_map/reduce_sum | solution.py:35
  28.5 6.0 %divide_convert_fusion = bf16[128,8,8,128]{3,2,1,0:T(8,128)(2,1)S(1)} fusion(f32[128,8,8]{2,1,0:T(8,128)S(1)} %fusion.13, f32[128,8,8,32]{3,2,1,0:T(8,128)S(1)} %get-tuple-element.65, f32[128,8,8]{2,1,0:T(8,128)S(1)} %get-tuple-element.64, pred[128,32]{1,0:T(8,128)(4,1)S(1)} %iota_compare_fusion, bf16[128,32,1024]{2,1,0:T(8,128)(2,1)} %param.14), kind=kOutput, calls=%fused_computation.14 | convolution fusion | flops 70254592 | bytes 11603968 | tf_op jit(solution)/shard_map/rkgp,rpkd->rkgd/dot_general | solution.py:36
  34.6 3.2 %copy.32 = bf16[16,8,64,128]{3,1,2,0:T(8,128)(2,1)} copy(bf16[16,8,64,128]{3,2,1,0:T(8,128)(2,1)S(1)} %bitcast.61) | data formatting | bytes 4194304
  38.9 1.6 copy-done.7
  41.6 2.0 %broadcast_select_fusion.1 = (bf16[64,4096]{1,0:T(8,128)(2,1)S(1)}, bf16[64,4096]{1,0:T(8,128)(2,1)S(1)}, bf16[64,4096]{1,0:T(8,128)(2,1)S(1)}, bf16[64,4096]{1,...) fusion(pred[]{:T(512)S(6)} %or.3, bf16[128,8192]{1,0:T(8,128)(2,1)} %bitcast.56, ...), kind=kLoop, calls=%fused_computation.55 | loop fusion | flops 524288 | bytes 5242893 | tf_op jit(solution)/shard_map/jit(_where)/select_n | solution.py:300
  45.1 1.8 collective-permute-start.7
  47.6 3.2 %collective-permute-start.3 = (bf16[64,4096]{1,0:T(8,128)(2,1)S(1)}, bf16[64,4096]{1,0:T(8,128)(2,1)}, u32[]{:S(2)}, u32[]{:S(2)}) collective-permute-start(bf16[64,4096]{1,0:T(8,128)(2,1)S(1)} %get-tuple-element.29), channel_id=1, source_target_pairs={{0,1},{1,0},{2,3},{3,2},{4,5},{5,4},{6,7},{7,6},{8,9},{9,8},{10,11... | collective-permute-start | bytes 1572872 | tf_op jit(solution)/shard_map/ppermute | solution.py:301
  50.8 9.1 %collective-permute-done.7 = bf16[64,4096]{1,0:T(8,128)(2,1)S(1)} collective-permute-done((bf16[64,4096]{1,0:T(8,128)(2,1)S(1)}, bf16[64,4096]{1,0:T(8,128)(2,1)S(1)}, u32[]{:S(2)}, u32[]{:S(2)}) %collective-permute-start.7) | collective-permute-done | bytes 524320 | tf_op jit(solution)/shard_map/ppermute | solution.py:301
  59.9 1.5 collective-permute-start.12
  61.4 2.7 %collective-permute-start.9 = (bf16[64,4096]{1,0:T(8,128)(2,1)S(1)}, bf16[64,4096]{1,0:T(8,128)(2,1)}, u32[]{:S(2)}, u32[]{:S(2)}) collective-permute-start(bf16[64,4096]{1,0:T(8,128)(2,1)S(1)} %broadcast_select_fusion), channel_id=1, source_target_pairs={{0,1},{1,0},{2,3},{3,2},{4,5},{5,4},{6,7},{7,6},{8,9},{9,8},{10,11... | collective-permute-start | bytes 1572872 | tf_op jit(solution)/shard_map/ppermute | solution.py:308
  65.9 5.4 %collective-permute-done.3 = bf16[64,4096]{1,0:T(8,128)(2,1)} collective-permute-done((bf16[64,4096]{1,0:T(8,128)(2,1)S(1)}, bf16[64,4096]{1,0:T(8,128)(2,1)}, u32[]{:S(2)}, u32[]{:S(2)}) %collective-permute-start.3) | collective-permute-done | bytes 524320 | tf_op jit(solution)/shard_map/ppermute | solution.py:301
  71.3 1.5 collective-permute-start.10
  72.7 2.7 %collective-permute-start.6 = (bf16[64,4096]{1,0:T(8,128)(2,1)}, bf16[64,4096]{1,0:T(8,128)(2,1)}, u32[]{:S(2)}, u32[]{:S(2)}) collective-permute-start(bf16[64,4096]{1,0:T(8,128)(2,1)} %broadcast_select_fusion.2), channel_id=1, source_target_pairs={{0,1},{1,0},{2,3},{3,2},{4,5},{5,4},{6,7},{7,6},{8,9},{9,8},{10,11... | collective-permute-start | bytes 1572872 | tf_op jit(solution)/shard_map/ppermute | solution.py:308
  76.6 7.3 %fusion.10.early_ref = f32[256,1024]{1,0:T(8,128)} fusion(bf16[8192,1024]{1,0:T(8,128)(2,1)} %param.16, s32[]{:T(128)S(6)} %select_n.106, bf16[128,4096]{1,0:T(8,128)(2,1)S(1)} %get-tuple-element.37, bf16[64,4096]{1,0:T(8,128)(2,1)S(1)} %collective-permute-done.7, bf16[64,4096]{1,0:T(8,128)(2,1)} %collective-permute-done.3), kind=kOutput, calls=%fused_computation.12 | convolution fusion | flops 2153775104 | bytes 11534340 | tf_op jit(solution)/shard_map/dot_general | solution.py:251
  83.9 1.5 collective-permute-start.18
  86.7 5.2 %all-to-all-start = ((bf16[2,4,64,3072]{3,2,1,0:T(8,128)(2,1)}), bf16[2,4,64,3072]{3,2,1,0:T(8,128)(2,1)}, u32[]{:S(2)}, u32[]{:S(2)}) async-start(bf16[2,4,64,3072]{3,2,1,0:T(8,128)(2,1)} %copy-done.4), calls=%async_computation | async-start | bytes 6291456 | tf_op jit(solution)/shard_map/all_to_all | solution.py:195
  91.9 1.8 collective-permute-done.6
  93.7 1.4 collective-permute-start.14
  95.2 1.5 collective-permute-start.15
  96.7 1.5 collective-permute-start.11
  98.2 2.0 %select_dynamic-update-slice_fusion.5 = bf16[512,4096]{1,0:T(8,128)(2,1)} fusion(bf16[512,4096]{1,0:T(8,128)(2,1)} %get-tuple-element.58, bf16[64,4096]{1,0:T(8,128)(2,1)} %collective-permute-done.3, bf16[64,4096]{1,0:T(8,128)(2,1)} %collective-permute-done.6, pred[]{:T(512)S(6)} %or.3), kind=kLoop, calls=%fused_computation.53 | loop fusion | flops 262144 | bytes 1572865
  100.2 2.0 %select_dynamic-update-slice_fusion.4 = bf16[512,4096]{1,0:T(8,128)(2,1)} fusion(bf16[512,4096]{1,0:T(8,128)(2,1)} %select_dynamic-update-slice_fusion.5, bf16[64,4096]{1,0:T(8,128)(2,1)} %copy-done.20, bf16[64,4096]{1,0:T(8,128)(2,1)} %collective-permute-done.9, pred[]{:T(512)S(6)} %or.3), kind=kLoop, calls=%fused_computation.52 | loop fusion | flops 262144 | bytes 1572865
  102.2 2.0 %select_dynamic-update-slice_fusion.3 = bf16[512,4096]{1,0:T(8,128)(2,1)} fusion(bf16[512,4096]{1,0:T(8,128)(2,1)} %select_dynamic-update-slice_fusion.4, bf16[64,4096]{1,0:T(8,128)(2,1)} %collective-permute-done.6, bf16[64,4096]{1,0:T(8,128)(2,1)} %copy-done.17, pred[]{:T(512)S(6)} %or.3), kind=kLoop, calls=%fused_computation.51 | loop fusion | flops 262144 | bytes 1572865
  104.1 1.9 %select_dynamic-update-slice_fusion.2 = bf16[512,4096]{1,0:T(8,128)(2,1)} fusion(bf16[512,4096]{1,0:T(8,128)(2,1)} %select_dynamic-update-slice_fusion.3, bf16[64,4096]{1,0:T(8,128)(2,1)} %collective-permute-done.9, bf16[64,4096]{1,0:T(8,128)(2,1)S(1)} %copy-done.16, pred[]{:T(512)S(6)} %or.3), kind=kLoop, calls=%fused_computation.50 | loop fusion | flops 262144 | bytes 1572865
  106.1 9.1 %collective-permute-done.11 = bf16[64,4096]{1,0:T(8,128)(2,1)S(1)} collective-permute-done((bf16[64,4096]{1,0:T(8,128)(2,1)}, bf16[64,4096]{1,0:T(8,128)(2,1)S(1)}, u32[]{:S(2)}, u32[]{:S(2)}) %collective-permute-start.11) | collective-permute-done | bytes 524320 | tf_op jit(solution)/shard_map/ppermute | solution.py:317
  115.2 1.5 collective-permute-start.17
  117.6 2.0 %select_dynamic-update-slice_fusion = bf16[512,4096]{1,0:T(8,128)(2,1)} fusion(bf16[512,4096]{1,0:T(8,128)(2,1)} %select_dynamic-update-slice_fusion.1, bf16[64,4096]{1,0:T(8,128)(2,1)} %collective-permute-done.13, bf16[64,4096]{1,0:T(8,128)(2,1)} %collective-permute-done.12, pred[]{:T(512)S(6)} %or.3), kind=kLoop, calls=%fused_computation.48 | loop fusion | flops 262144 | bytes 1572865 | tf_op jit(solution)/shard_map/concatenate | solution.py:321
  119.6 3.2 %constant_dynamic-slice_fusion.4 = bf16[512,2048]{1,0:T(8,128)(2,1)} fusion(bf16[512,4096]{1,0:T(8,128)(2,1)} %select_dynamic-update-slice_fusion, s32[]{:T(128)S(6)} %select_n.118), kind=kLoop, calls=%fused_computation.68 | loop fusion | bytes 4194308 | tf_op jit(solution)/shard_map/dynamic_slice | solution.py:333
  122.8 4.1 %all-to-all-done.fetched_ref = bf16[2,4,64,3072]{3,2,1,0:T(8,128)(2,1)} async-done(((bf16[2,4,64,3072]{3,2,1,0:T(8,128)(2,1)}), bf16[2,4,64,3072]{3,2,1,0:T(8,128)(2,1)}, u32[]{:S(2)}, u32[]{:S(2)}) %all-to-all-start) | async-done | bytes 3145760 | tf_op jit(solution)/shard_map/all_to_all | solution.py:195
  126.9 1.4 copy-done.3
  128.3 2.0 %shard_map.120.refs_4_ = bf16[4,64,3072]{2,1,0:T(8,128)(2,1)S(1)} custom-call(s32[1]{0:T(128)} %bitcast.2.here_ref, s32[4,4]{1,0:T(4,128)S(1)} %pad_add_fusion.ids_ref, s32[48]{0:T(128)S(1)} %copy-done.9, s32[4]{0:T(128)S(1)} %fusion.49.order_ref, bf16[12,64,2048]{2,1,0:T(8,128)(2,1)S(1)} %bitcast.55, bf16[12,64,1024]{2,1,0:T(8,128)(2,1)S(1)} %copy-done.3, ...), custom_call_target="tpu_custom_call" | custom-call | tf_op jit(solution)/shard_map/pallas_call | solution.py:203
  132.8 3.0 %collective-permute-start.21 = (f32[4,64,128]{2,1,0:T(8,128)S(1)}, f32[4,64,128]{2,1,0:T(8,128)S(1)}, u32[]{:S(2)}, u32[]{:S(2)}) collective-permute-start(f32[4,64,128]{2,1,0:T(8,128)S(1)} %gather_fusion), channel_id=1, source_target_pairs={{0,1},{1,0},{2,3},{3,2},{4,5},{5,4},{6,7},{7,6},{8,9},{9,8},{10,11... | collective-permute-start | bytes 393224 | tf_op jit(solution)/shard_map/ppermute | solution.py:218
  135.8 8.1 %fusion.6.near_ref = f32[512,1024]{1,0:T(8,128)S(1)} fusion(bf16[512,4096]{1,0:T(8,128)(2,1)} %select_dynamic-update-slice_fusion, bf16[8192,1024]{1,0:T(8,128)(2,1)} %param.16, s32[]{:T(128)S(6)} %select_n.104), kind=kOutput, calls=%fused_computation.8 | convolution fusion | flops 4294967296 | bytes 14680068 | tf_op jit(solution)/shard_map/dot_general | solution.py:251
  145.0 2.3 %pad_maximum_fusion.2 = bf16[128,4096]{1,0:T(8,128)(2,1)} fusion(bf16[64,4096]{1,0:T(8,128)(2,1)} %collective-permute-done.15, bf16[64,4096]{1,0:T(8,128)(2,1)} %collective-permute-done.14), kind=kLoop, calls=%fused_computation.43 | loop fusion | flops 2097152 | bytes 2097152 | tf_op jit(solution)/shard_map/concatenate | solution.py:345
  147.3 3.6 %collective-permute-done.22 = f32[4,64,128]{2,1,0:T(8,128)S(1)} collective-permute-done((f32[4,64,128]{2,1,0:T(8,128)S(1)}, f32[4,64,128]{2,1,0:T(8,128)S(1)}, u32[]{:S(2)}, u32[]{:S(2)}) %collective-permute-start.22) | collective-permute-done | bytes 131104 | tf_op jit(solution)/shard_map/ppermute | solution.py:218
  151.5 6.5 %fusion.33 = bf16[256,1024]{1,0:T(8,128)(2,1)S(1)} fusion(bf16[4096,1024]{1,0:T(8,128)(2,1)} %all-gather.2.cloned.1.call-done, bf16[128,4096]{1,0:T(8,128)(2,1)} %copy-done.18, bf16[64,4096]{1,0:T(8,128)(2,1)} %collective-permute-done.15, bf16[64,4096]{1,0:T(8,128)(2,1)} %collective-permute-done.14), kind=kOutput, calls=%fused_computation.39 | convolution fusion | flops 2154037248 | bytes 11010048 | tf_op jit(solution)/shard_map/dot_general | solution.py:251
  158.0 1.6 collective-permute-start.19
  159.6 3.4 %convolution_convert_fusion = bf16[128,1024]{1,0:T(8,128)(2,1)S(1)} fusion(bf16[4096,1024]{1,0:T(8,128)(2,1)S(1)} %copy-done.22, bf16[64,4096]{1,0:T(8,128)(2,1)} %collective-permute-done.18, bf16[64,4096]{1,0:T(8,128)(2,1)} %collective-permute-done.17), kind=kOutput, calls=%fused_computation.40 | convolution fusion | flops 1075970048 | bytes 9699328 | tf_op jit(solution)/shard_map/dot_general | solution.py:251
  163.1 1.4 collective-permute-start.20
  164.5 3.6 %fusion.8.late_ref = f32[256,1024]{1,0:T(8,128)S(1)} fusion(bf16[8192,1024]{1,0:T(8,128)(2,1)S(1)} %bitcast.63, s32[]{:T(128)S(6)} %select_n.106, bf16[64,4096]{1,0:T(8,128)(2,1)} %collective-permute-done.18, bf16[64,4096]{1,0:T(8,128)(2,1)} %collective-permute-done.17, bf16[128,4096]{1,0:T(8,128)(2,1)S(1)} %copy-done.19), kind=kOutput, calls=%fused_computation.10 | convolution fusion | flops 2153775104 | bytes 11534340 | tf_op jit(solution)/shard_map/dot_general | solution.py:251
  168.1 4.6 %collective-permute-done.19 = bf16[256,1024]{1,0:T(8,128)(2,1)S(1)} collective-permute-done((bf16[256,1024]{1,0:T(8,128)(2,1)S(1)}, bf16[256,1024]{1,0:T(8,128)(2,1)S(1)}, u32[]{:S(2)}, u32[]{:S(2)}) %collective-permute-start.19) | collective-permute-done | bytes 524320 | tf_op jit(solution)/shard_map/ppermute | solution.py:347
  172.8 2.8 %collective-permute-done.20.refs_2_ = bf16[128,1024]{1,0:T(8,128)(2,1)S(1)} collective-permute-done((bf16[128,1024]{1,0:T(8,128)(2,1)S(1)}, bf16[128,1024]{1,0:T(8,128)(2,1)S(1)}, u32[]{:S(2)}, u32[]{:S(2)}) %collective-permute-start.20) | collective-permute-done | bytes 262176 | tf_op jit(solution)/shard_map/ppermute | solution.py:351
  175.6 2.2 %shard_map.121 = bf16[512,1024]{1,0:T(8,128)(2,1)} custom-call(s32[4]{0:T(128)S(1)} %fusion.49.order_ref, s32[4]{0:T(128)S(1)} %copy-done.10, s32[1]{0:T(128)} %bitcast.1.end_ref, f32[512,1024]{1,0:T(8,128)S(1)} %fusion.6.near_ref, f32[256,1024]{1,0:T(8,128)S(1)} %copy-done.8, f32[256,1024]{1,0:T(8,128)S(1)} %fusion.8.late_ref, ...), custom_call_target="tpu_custom_call" | custom-call | tf_op jit(solution)/shard_map/pallas_call | solution.py:354
  (100 shorter events, 15.4 us)
Async XLA Ops:
  6.5 144.9 %all-gather.2.cloned.1.call-start = ((), (), s32[]{:S(2)}) async-start(), calls=%async_computation.1 | async-start | bytes 9437184 | tf_op jit(solution)/shard_map/all_gather | solution.py:293
  6.5 31.2 %collective-permute-start = (s32[4]{0:T(128)}, s32[4]{0:T(128)S(1)}, u32[]{:S(2)}, u32[]{:S(2)}) collective-permute-start(s32[4]{0:T(128)} %param.19), channel_id=1, source_target_pairs={{0,12},{4,0},{8,4},{12,8},{1,13},{5,1},{9,5},{13,9},{2,14},{6,2},{... | collective-permute-start | bytes 56 | tf_op jit(solution)/shard_map/ppermute | solution.py:160
  8.9 28.8 %collective-permute-start.1 = (s32[4]{0:T(128)}, s32[4]{0:T(128)S(1)}, u32[]{:S(2)}, u32[]{:S(2)}) collective-permute-start(s32[4]{0:T(128)} %param.19), channel_id=1, source_target_pairs={{0,8},{4,12},{8,0},{12,4},{1,9},{5,13},{9,1},{13,5},{2,10},{6,14},... | collective-permute-start | bytes 56 | tf_op jit(solution)/shard_map/ppermute | solution.py:160
  9.5 28.3 %collective-permute-start.2 = (s32[4]{0:T(128)}, s32[4]{0:T(128)S(1)}, u32[]{:S(2)}, u32[]{:S(2)}) collective-permute-start(s32[4]{0:T(128)} %param.19), channel_id=1, source_target_pairs={{0,4},{4,8},{8,12},{12,0},{1,5},{5,9},{9,13},{13,1},{2,6},{6,10},{... | collective-permute-start | bytes 56 | tf_op jit(solution)/shard_map/ppermute | solution.py:160
  11.0 29.5 %collective-permute-start.16 = (bf16[512,1024]{1,0:T(8,128)(2,1)S(1)}, bf16[512,1024]{1,0:T(8,128)(2,1)}, u32[]{:S(2)}, u32[]{:S(2)}) collective-permute-start(bf16[512,1024]{1,0:T(8,128)(2,1)S(1)} %constant_dynamic-slice_fusion.3), channel_id=1, source_target_pairs={{0,1},{3,2},{4,5},{7,6},{8,9},{11,10},{12,13},{15,14},{16,17},{19,... | collective-permute-start | bytes 3145736 | tf_op jit(solution)/shard_map/ppermute | solution.py:286
  28.5 9.3 %copy-start.1 = (bf16[12,64,1024]{2,1,0:T(8,128)(2,1)S(1)}, bf16[12,64,1024]{2,1,0:T(8,128)(2,1)}, u32[]{:S(2)}) copy-start(bf16[12,64,1024]{2,1,0:T(8,128)(2,1)} %up_ref.5) | copy-start | bytes 4718596
  34.5 3.3 %copy-start = (bf16[12,2048,64]{1,2,0:T(8,128)(2,1)S(1)}, bf16[12,2048,64]{1,2,0:T(8,128)(2,1)}, u32[]{:S(2)}) copy-start(bf16[12,2048,64]{1,2,0:T(8,128)(2,1)} %param.17) | copy-start | bytes 9437188
  34.5 3.3 %copy-start.9 = (s32[48]{0:T(128)S(1)}, s32[48]{0:T(128)}, u32[]{:S(2)}) copy-start(s32[48]{0:T(128)} %slots_ref.5) | copy-start | bytes 580
  40.5 3.8 %copy-start.23 = (s32[4,4]{1,0:T(4,128)S(1)}, s32[4,4]{1,0:T(4,128)}, u32[]{:S(2)}) copy-start(s32[4,4]{1,0:T(4,128)} %constant.65.clone) | copy-start | bytes 196
  40.5 23.6 %collective-permute-start.5 = (bf16[2,4,64,3072]{3,2,1,0:T(8,128)(2,1)}, bf16[2,4,64,3072]{3,2,1,0:T(8,128)(2,1)}, u32[]{:S(2)}, u32[]{:S(2)}) collective-permute-start(bf16[2,4,64,3072]{3,2,1,0:T(8,128)(2,1)} %copy-done.7), channel_id=1, source_target_pairs={{0,4},{4,0},{8,12},{12,8},{1,5},{5,1},{9,13},{13,9},{2,6},{6,2},{1... | collective-permute-start | bytes 9437192 | tf_op jit(solution)/shard_map/ppermute | solution.py:180
  41.6 22.5 %copy-start.2 = (bf16[12,64,1024]{2,1,0:T(8,128)(2,1)S(1)}, bf16[12,64,1024]{2,1,0:T(8,128)(2,1)}, u32[]{:S(2)}) copy-start(bf16[12,64,1024]{2,1,0:T(8,128)(2,1)} %up_ref.5) | copy-start | bytes 4718596
  43.6 20.5 %copy-start.13 = (bf16[64,4096]{1,0:T(8,128)(2,1)}, bf16[64,4096]{1,0:T(8,128)(2,1)S(1)}, u32[]{:S(2)}) copy-start(bf16[64,4096]{1,0:T(8,128)(2,1)S(1)} %get-tuple-element.46) | copy-start | bytes 1572868
  43.6 21.3 %copy-start.14 = (bf16[64,4096]{1,0:T(8,128)(2,1)}, bf16[64,4096]{1,0:T(8,128)(2,1)S(1)}, u32[]{:S(2)}) copy-start(bf16[64,4096]{1,0:T(8,128)(2,1)S(1)} %get-tuple-element.45) | copy-start | bytes 1572868
  43.6 7.1 %collective-permute-start.8 = (bf16[64,4096]{1,0:T(8,128)(2,1)S(1)}, bf16[64,4096]{1,0:T(8,128)(2,1)S(1)}, u32[]{:S(2)}, u32[]{:S(2)}) collective-permute-start(bf16[64,4096]{1,0:T(8,128)(2,1)S(1)} %get-tuple-element.35), channel_id=1, source_target_pairs={{1,2},{2,1},{5,6},{6,5},{9,10},{10,9},{13,14},{14,13},{17,18},{18,... | collective-permute-start | bytes 1572872 | tf_op jit(solution)/shard_map/ppermute | solution.py:302
  45.1 14.8 %collective-permute-start.7 = (bf16[64,4096]{1,0:T(8,128)(2,1)S(1)}, bf16[64,4096]{1,0:T(8,128)(2,1)S(1)}, u32[]{:S(2)}, u32[]{:S(2)}) collective-permute-start(bf16[64,4096]{1,0:T(8,128)(2,1)S(1)} %get-tuple-element.34), channel_id=1, source_target_pairs={{0,1},{1,0},{2,3},{3,2},{4,5},{5,4},{6,7},{7,6},{8,9},{9,8},{10,11... | collective-permute-start | bytes 1572872 | tf_op jit(solution)/shard_map/ppermute | solution.py:301
  46.9 18.0 %collective-permute-start.4 = (bf16[64,4096]{1,0:T(8,128)(2,1)S(1)}, bf16[64,4096]{1,0:T(8,128)(2,1)S(1)}, u32[]{:S(2)}, u32[]{:S(2)}) collective-permute-start(bf16[64,4096]{1,0:T(8,128)(2,1)S(1)} %get-tuple-element.30), channel_id=1, source_target_pairs={{1,2},{2,1},{5,6},{6,5},{9,10},{10,9},{13,14},{14,13},{17,18},{18,... | collective-permute-start | bytes 1572872 | tf_op jit(solution)/shard_map/ppermute | solution.py:302
  47.6 23.7 %collective-permute-start.3 = (bf16[64,4096]{1,0:T(8,128)(2,1)S(1)}, bf16[64,4096]{1,0:T(8,128)(2,1)}, u32[]{:S(2)}, u32[]{:S(2)}) collective-permute-start(bf16[64,4096]{1,0:T(8,128)(2,1)S(1)} %get-tuple-element.29), channel_id=1, source_target_pairs={{0,1},{1,0},{2,3},{3,2},{4,5},{5,4},{6,7},{7,6},{8,9},{9,8},{10,11... | collective-permute-start | bytes 1572872 | tf_op jit(solution)/shard_map/ppermute | solution.py:301
  50.7 13.4 %copy-start.15 = (bf16[64,4096]{1,0:T(8,128)(2,1)}, bf16[64,4096]{1,0:T(8,128)(2,1)S(1)}, u32[]{:S(2)}) copy-start(bf16[64,4096]{1,0:T(8,128)(2,1)S(1)} %collective-permute-done.8) | copy-start | bytes 1572868
  50.8 24.6 %copy-start.11 = (bf16[16,8,64,128]{3,1,2,0:T(8,128)(2,1)S(1)}, bf16[16,8,64,128]{3,1,2,0:T(8,128)(2,1)}, u32[]{:S(2)}) copy-start(bf16[16,8,64,128]{3,1,2,0:T(8,128)(2,1)} %copy.32) | copy-start | bytes 6291460
  59.9 16.7 %copy-start.20 = (bf16[64,4096]{1,0:T(8,128)(2,1)}, bf16[64,4096]{1,0:T(8,128)(2,1)S(1)}, u32[]{:S(2)}) copy-start(bf16[64,4096]{1,0:T(8,128)(2,1)S(1)} %collective-permute-done.7) | copy-start | bytes 1572868
  59.9 25.4 %collective-permute-start.12 = (bf16[64,4096]{1,0:T(8,128)(2,1)S(1)}, bf16[64,4096]{1,0:T(8,128)(2,1)}, u32[]{:S(2)}, u32[]{:S(2)}) collective-permute-start(bf16[64,4096]{1,0:T(8,128)(2,1)S(1)} %collective-permute-done.7), channel_id=1, source_target_pairs={{1,2},{2,1},{5,6},{6,5},{9,10},{10,9},{13,14},{14,13},{17,18},{18,... | collective-permute-start | bytes 1572872 | tf_op jit(solution)/shard_map/ppermute | solution.py:309
  61.4 22.5 %collective-permute-start.9 = (bf16[64,4096]{1,0:T(8,128)(2,1)S(1)}, bf16[64,4096]{1,0:T(8,128)(2,1)}, u32[]{:S(2)}, u32[]{:S(2)}) collective-permute-start(bf16[64,4096]{1,0:T(8,128)(2,1)S(1)} %broadcast_select_fusion), channel_id=1, source_target_pairs={{0,1},{1,0},{2,3},{3,2},{4,5},{5,4},{6,7},{7,6},{8,9},{9,8},{10,11... | collective-permute-start | bytes 1572872 | tf_op jit(solution)/shard_map/ppermute | solution.py:308
  64.9 19.0 %copy-start.4 = (bf16[2,4,64,3072]{3,2,1,0:T(8,128)(2,1)}, bf16[2,4,64,3072]{3,2,1,0:T(8,128)(2,1)S(1)}, u32[]{:S(2)}) copy-start(bf16[2,4,64,3072]{3,2,1,0:T(8,128)(2,1)S(1)} %shard_map.119) | copy-start | bytes 9437188
  64.9 19.0 %copy-start.17 = (bf16[64,4096]{1,0:T(8,128)(2,1)}, bf16[64,4096]{1,0:T(8,128)(2,1)S(1)}, u32[]{:S(2)}) copy-start(bf16[64,4096]{1,0:T(8,128)(2,1)S(1)} %collective-permute-done.4) | copy-start | bytes 1572868
  71.3 20.6 %collective-permute-start.10 = (bf16[64,4096]{1,0:T(8,128)(2,1)}, bf16[64,4096]{1,0:T(8,128)(2,1)}, u32[]{:S(2)}, u32[]{:S(2)}) collective-permute-start(bf16[64,4096]{1,0:T(8,128)(2,1)} %collective-permute-done.3), channel_id=1, source_target_pairs={{1,2},{2,1},{5,6},{6,5},{9,10},{10,9},{13,14},{14,13},{17,18},{18,... | collective-permute-start | bytes 1572872 | tf_op jit(solution)/shard_map/ppermute | solution.py:309
  72.7 21.0 %collective-permute-start.6 = (bf16[64,4096]{1,0:T(8,128)(2,1)}, bf16[64,4096]{1,0:T(8,128)(2,1)}, u32[]{:S(2)}, u32[]{:S(2)}) collective-permute-start(bf16[64,4096]{1,0:T(8,128)(2,1)} %broadcast_select_fusion.2), channel_id=1, source_target_pairs={{0,1},{1,0},{2,3},{3,2},{4,5},{5,4},{6,7},{7,6},{8,9},{9,8},{10,11... | collective-permute-start | bytes 1572872 | tf_op jit(solution)/shard_map/ppermute | solution.py:308
  76.6 7.3 %copy-start.18 = (bf16[128,4096]{1,0:T(8,128)(2,1)}, bf16[128,4096]{1,0:T(8,128)(2,1)S(1)}, u32[]{:S(2)}) copy-start(bf16[128,4096]{1,0:T(8,128)(2,1)S(1)} %get-tuple-element.37) | copy-start | bytes 3145732
  83.9 75.7 %collective-permute-start.18 = (bf16[64,4096]{1,0:T(8,128)(2,1)}, bf16[64,4096]{1,0:T(8,128)(2,1)}, u32[]{:S(2)}, u32[]{:S(2)}) collective-permute-start(bf16[64,4096]{1,0:T(8,128)(2,1)} %collective-permute-done.9), channel_id=1, source_target_pairs={{1,2},{2,1},{5,6},{6,5},{9,10},{10,9},{13,14},{14,13},{17,18},{18,... | collective-permute-start | bytes 1572872 | tf_op jit(solution)/shard_map/ppermute | solution.py:319
  85.4 32.2 %collective-permute-start.13 = (bf16[64,4096]{1,0:T(8,128)(2,1)}, bf16[64,4096]{1,0:T(8,128)(2,1)}, u32[]{:S(2)}, u32[]{:S(2)}) collective-permute-start(bf16[64,4096]{1,0:T(8,128)(2,1)} %collective-permute-done.12), channel_id=1, source_target_pairs={{1,0},{2,3},{5,4},{6,7},{9,8},{10,11},{13,12},{14,15},{17,16},{18,... | collective-permute-start | bytes 1572872 | tf_op jit(solution)/shard_map/ppermute | solution.py:317
  86.7 40.2 %all-to-all-start = ((bf16[2,4,64,3072]{3,2,1,0:T(8,128)(2,1)}), bf16[2,4,64,3072]{3,2,1,0:T(8,128)(2,1)}, u32[]{:S(2)}, u32[]{:S(2)}) async-start(bf16[2,4,64,3072]{3,2,1,0:T(8,128)(2,1)} %copy-done.4), calls=%async_computation | async-start | bytes 6291456 | tf_op jit(solution)/shard_map/all_to_all | solution.py:195
  91.9 12.3 %copy-start.16 = (bf16[64,4096]{1,0:T(8,128)(2,1)S(1)}, bf16[64,4096]{1,0:T(8,128)(2,1)}, u32[]{:S(2)}) copy-start(bf16[64,4096]{1,0:T(8,128)(2,1)} %copy-done.15) | copy-start | bytes 1572868
  93.7 51.3 %collective-permute-start.14 = (bf16[64,4096]{1,0:T(8,128)(2,1)}, bf16[64,4096]{1,0:T(8,128)(2,1)}, u32[]{:S(2)}, u32[]{:S(2)}) collective-permute-start(bf16[64,4096]{1,0:T(8,128)(2,1)} %copy-done.14), channel_id=1, source_target_pairs={{1,2},{2,1},{5,6},{6,5},{9,10},{10,9},{13,14},{14,13},{17,18},{18,... | collective-permute-start | bytes 1572872 | tf_op jit(solution)/shard_map/ppermute | solution.py:318
  95.2 49.8 %collective-permute-start.15 = (bf16[64,4096]{1,0:T(8,128)(2,1)}, bf16[64,4096]{1,0:T(8,128)(2,1)}, u32[]{:S(2)}, u32[]{:S(2)}) collective-permute-start(bf16[64,4096]{1,0:T(8,128)(2,1)} %copy-done.13), channel_id=1, source_target_pairs={{1,2},{2,1},{5,6},{6,5},{9,10},{10,9},{13,14},{14,13},{17,18},{18,... | collective-permute-start | bytes 1572872 | tf_op jit(solution)/shard_map/ppermute | solution.py:318
  96.7 18.5 %collective-permute-start.11 = (bf16[64,4096]{1,0:T(8,128)(2,1)}, bf16[64,4096]{1,0:T(8,128)(2,1)S(1)}, u32[]{:S(2)}, u32[]{:S(2)}) collective-permute-start(bf16[64,4096]{1,0:T(8,128)(2,1)} %collective-permute-done.10), channel_id=1, source_target_pairs={{1,0},{2,3},{5,4},{6,7},{9,8},{10,11},{13,12},{14,15},{17,16},{18,... | collective-permute-start | bytes 1572872 | tf_op jit(solution)/shard_map/ppermute | solution.py:317
  115.2 44.4 %collective-permute-start.17 = (bf16[64,4096]{1,0:T(8,128)(2,1)}, bf16[64,4096]{1,0:T(8,128)(2,1)}, u32[]{:S(2)}, u32[]{:S(2)}) collective-permute-start(bf16[64,4096]{1,0:T(8,128)(2,1)} %collective-permute-done.6), channel_id=1, source_target_pairs={{1,2},{2,1},{5,6},{6,5},{9,10},{10,9},{13,14},{14,13},{17,18},{18,... | collective-permute-start | bytes 1572872 | tf_op jit(solution)/shard_map/ppermute | solution.py:319
  132.8 11.2 %collective-permute-start.21 = (f32[4,64,128]{2,1,0:T(8,128)S(1)}, f32[4,64,128]{2,1,0:T(8,128)S(1)}, u32[]{:S(2)}, u32[]{:S(2)}) collective-permute-start(f32[4,64,128]{2,1,0:T(8,128)S(1)} %gather_fusion), channel_id=1, source_target_pairs={{0,1},{1,0},{2,3},{3,2},{4,5},{5,4},{6,7},{7,6},{8,9},{9,8},{10,11... | collective-permute-start | bytes 393224 | tf_op jit(solution)/shard_map/ppermute | solution.py:218
  144.0 6.8 %collective-permute-start.22 = (f32[4,64,128]{2,1,0:T(8,128)S(1)}, f32[4,64,128]{2,1,0:T(8,128)S(1)}, u32[]{:S(2)}, u32[]{:S(2)}) collective-permute-start(f32[4,64,128]{2,1,0:T(8,128)S(1)} %add.64), channel_id=1, source_target_pairs={{0,2},{1,3},{2,0},{3,1},{4,6},{5,7},{6,4},{7,5},{8,10},{9,11},{10,... | collective-permute-start | bytes 393224 | tf_op jit(solution)/shard_map/ppermute | solution.py:218
  151.5 8.2 %copy-start.22 = (bf16[4096,1024]{1,0:T(8,128)(2,1)S(1)}, bf16[4096,1024]{1,0:T(8,128)(2,1)}, u32[]{:S(2)}) copy-start(bf16[4096,1024]{1,0:T(8,128)(2,1)} %all-gather.2.cloned.1.call-done) | copy-start | bytes 25165828
  151.5 13.0 %slice-start = ((s8[16777216]{0:T(1024)(128)(4,1)}), s8[4194304]{0:T(1024)(128)(4,1)S(1)}, s32[]{:S(2)}) async-start(s8[16777216]{0:T(1024)(128)(4,1)} %bitcast.62), calls=%async_computation.2 | async-start | bytes 8388608
  151.5 13.0 %slice-start.1 = ((s8[16777216]{0:T(1024)(128)(4,1)}), s8[4194304]{0:T(1024)(128)(4,1)S(1)}, s32[]{:S(2)}) async-start(s8[16777216]{0:T(1024)(128)(4,1)} %bitcast.62), calls=%async_computation.3 | async-start | bytes 8388608
  151.5 13.0 %slice-start.2 = ((s8[16777216]{0:T(1024)(128)(4,1)}), s8[4194304]{0:T(1024)(128)(4,1)S(1)}, s32[]{:S(2)}) async-start(s8[16777216]{0:T(1024)(128)(4,1)} %bitcast.62), calls=%async_computation.4 | async-start | bytes 8388608
  158.0 6.5 %copy-start.19 = (bf16[128,4096]{1,0:T(8,128)(2,1)S(1)}, bf16[128,4096]{1,0:T(8,128)(2,1)}, u32[]{:S(2)}) copy-start(bf16[128,4096]{1,0:T(8,128)(2,1)} %pad_maximum_fusion.2) | copy-start | bytes 3145732
  158.0 6.5 %slice-start.3 = ((s8[16777216]{0:T(1024)(128)(4,1)}), s8[4194304]{0:T(1024)(128)(4,1)S(1)}, s32[]{:S(2)}) async-start(s8[16777216]{0:T(1024)(128)(4,1)} %bitcast.62), calls=%async_computation.5 | async-start | bytes 8388608
  158.0 14.7 %collective-permute-start.19 = (bf16[256,1024]{1,0:T(8,128)(2,1)S(1)}, bf16[256,1024]{1,0:T(8,128)(2,1)S(1)}, u32[]{:S(2)}, u32[]{:S(2)}) collective-permute-start(bf16[256,1024]{1,0:T(8,128)(2,1)S(1)} %fusion.33), channel_id=1, source_target_pairs={{1,0},{2,3},{5,4},{6,7},{9,8},{10,11},{13,12},{14,15},{17,16},{18,... | collective-permute-start | bytes 1572872 | tf_op jit(solution)/shard_map/ppermute | solution.py:347
  163.0 12.5 %copy-start.6 = (bf16[4,64,3072]{2,1,0:T(8,128)(2,1)S(1)}, bf16[4,64,3072]{2,1,0:T(8,128)(2,1)}, u32[]{:S(2)}) copy-start(bf16[4,64,3072]{2,1,0:T(8,128)(2,1)} %copy-done.5) | copy-start | bytes 4718596
  163.0 12.5 %copy-start.8 = (f32[256,1024]{1,0:T(8,128)S(1)}, f32[256,1024]{1,0:T(8,128)}, u32[]{:S(2)}) copy-start(f32[256,1024]{1,0:T(8,128)} %fusion.10.early_ref) | copy-start | bytes 3145732
  163.0 12.5 %copy-start.10 = (s32[4]{0:T(128)S(1)}, s32[4]{0:T(128)}, u32[]{:S(2)}) copy-start(s32[4]{0:T(128)} %live_ref.1) | copy-start | bytes 52
  163.1 12.5 %collective-permute-start.20 = (bf16[128,1024]{1,0:T(8,128)(2,1)S(1)}, bf16[128,1024]{1,0:T(8,128)(2,1)S(1)}, u32[]{:S(2)}, u32[]{:S(2)}) collective-permute-start(bf16[128,1024]{1,0:T(8,128)(2,1)S(1)} %convolution_convert_fusion), channel_id=1, source_target_pairs={{1,0},{2,3},{5,4},{6,7},{9,8},{10,11},{13,12},{14,15},{17,16},{18,... | collective-permute-start | bytes 786440 | tf_op jit(solution)/shard_map/ppermute | solution.py:351
  (5 other events, 9.4 us)
Sparse Core Ops, SparseCore 0:
  40.6 54.3 all-gather.1
